TPU v7x, 512 devices: a whole 4x4x16 slice. The times are simulated.
512 devices in a mesh: plane: 64 (over z, x_lo, core), tower: 8 (over x_hi, y).
Axes of the slice: x: 4 (x_hi: 2, x_lo: 2; x = x_hi * 2 + x_lo), y: 4, z: 16, core: 2. Of those that a mesh axis runs over, the one named last changes fastest.
Arguments:
- offsets: bfloat16 [64, 16, 3, 128], P('plane', 'tower'), may hold values from 0 to 1, as said below
- features: bfloat16 [64, 16, 128, 256], P('plane', 'tower'), may hold values from -6 to 6
- cotangent: bfloat16 [64, 16, 128, 256], P('plane', 'tower'), may hold values from -6 to 6
- w_in: bfloat16 [256, 256], replicated, may hold values from -0.375 to 0.375
- w_out: bfloat16 [256, 256], replicated, may hold values from -0.375 to 0.375
- w_filter: bfloat16 [8, 256], replicated, may hold values from -2 to 2
- counts: int32 [64, 16], P('plane', 'tower'), may hold values from 64 to 128
Outputs:
- forces: float32 [64, 16, 3, 128], P('plane', 'tower')
Inputs may be any that keep to these rules, and one draw needn't show every extreme that they name: offsets lie in the unit box.
All inputs are finite; a program needn't handle non-finite values.
Results may differ from a plain program's by a relative error of at most 0.005.
Values may be sent and summed in bfloat16 or wider, within the bound.
No kernel may reach another device: no remote copies, remote signals or barrier semaphores. Data moves between devices by JAX's collectives and lax.ppermute only.
A program may use at most 64 MiB of HBM per device.

v0:
```python
import jax
import jax.numpy as jnp
from jax import lax
from jax.sharding import PartitionSpec as P

PITCH = 12.5
CUTOFF_SQUARED = 25.0
CENTER_STEP = 3.125
GAMMA = 0.2
FORCE_UNIT = 0.005


def extended(cells, sides, width):
    for axis, dim in sides:
        count = lax.axis_size(axis)
        head = lax.slice_in_dim(cells, 0, width, axis=dim)
        tail = lax.slice_in_dim(cells, cells.shape[dim] - width, cells.shape[dim], axis=dim)
        cells = jnp.concatenate(
            [
                lax.ppermute(tail, axis, [(i, (i + 1) % count) for i in range(count)]),
                cells,
                lax.ppermute(head, axis, [((i + 1) % count, i) for i in range(count)]),
            ],
            axis=dim,
        )
    return cells


def pair_forces(first, second, plane_step, box_step, w_filter):
    first_units = first[0].astype(jnp.float32)
    second_units = second[0].astype(jnp.float32)
    atoms = first_units.shape[1]
    radial = w_filter.shape[0]
    width = w_filter.shape[1]
    centers = CENTER_STEP * jnp.arange(radial).astype(jnp.float32)
    along_x = (plane_step + second_units[0][None, :] - first_units[0][:, None]) * PITCH
    along_y = (box_step + second_units[1][None, :] - first_units[1][:, None]) * PITCH
    along_z = (second_units[2][None, :] - first_units[2][:, None]) * PITCH
    squared = along_x * along_x + along_y * along_y + along_z * along_z
    margin = jnp.maximum(1.0 - squared / CUTOFF_SQUARED, 0.0)
    spread = squared[:, None, :] - centers[None, :, None]
    decays = jnp.exp(-GAMMA * spread * spread)
    slopes = decays * (
        -2.0 * GAMMA * spread * (margin * margin)[:, None, :]
        - 2.0 * margin[:, None, :] / CUTOFF_SQUARED
    )
    filtered = (first[2][:, None, :] * w_filter[None, :, :]).reshape(atoms * radial, width)
    forward = lax.dot_general(
        filtered, second[1], (((1,), (1,)), ((), ())), preferred_element_type=jnp.float32
    )
    strength = jnp.sum(slopes * forward.reshape(atoms, radial, atoms), axis=1)
    filtered_back = (second[2][:, None, :] * w_filter[None, :, :]).reshape(atoms * radial, width)
    backward = lax.dot_general(
        filtered_back, first[1], (((1,), (1,)), ((), ())), preferred_element_type=jnp.float32
    )
    slopes_back = jnp.transpose(slopes, (2, 1, 0))
    strength = strength + jnp.transpose(
        jnp.sum(slopes_back * backward.reshape(atoms, radial, atoms), axis=1)
    )
    first_force = (
        2.0
        * FORCE_UNIT
        * jnp.stack(
            [
                jnp.sum(strength * along_x, 1),
                jnp.sum(strength * along_y, 1),
                jnp.sum(strength * along_z, 1),
            ]
        )
    )
    second_force = (
        -2.0
        * FORCE_UNIT
        * jnp.stack(
            [
                jnp.sum(strength * along_x, 0),
                jnp.sum(strength * along_y, 0),
                jnp.sum(strength * along_z, 0),
            ]
        )
    )
    return (first_force, second_force)


def on_device(offsets, features, cotangent, w_in, w_out, w_filter, counts):
    per_dev = offsets.shape[1]
    box_atoms = offsets.shape[3]
    width = features.shape[3]
    slots = jnp.arange(box_atoms, dtype=jnp.int32)
    live = (slots[None, :] < counts[0][:, None])[:, :, None]
    values = jnp.dot(
        features[0].reshape(per_dev * box_atoms, width), w_in, preferred_element_type=jnp.float32
    )
    values = jnp.where(live, values.reshape(per_dev, box_atoms, width), 0.0).astype(jnp.bfloat16)
    grads = lax.dot_general(
        cotangent[0].reshape(per_dev * box_atoms, width),
        w_out,
        (((1,), (1,)), ((), ())),
        preferred_element_type=jnp.float32,
    )
    grads = jnp.where(live, grads.reshape(per_dev, box_atoms, width), 0.0).astype(jnp.bfloat16)
    ext_units, ext_values, ext_grads = (
        extended(offsets, (("plane", 0), ("tower", 1)), 1),
        extended(values[None], (("plane", 0), ("tower", 1)), 1),
        extended(grads[None], (("plane", 0), ("tower", 1)), 1),
    )
    force_rows = []
    for own_index in range(per_dev):
        own = (offsets[0, own_index], values[own_index], grads[own_index])
        summed = jnp.zeros((3, box_atoms), jnp.float32)
        for across in range(3):
            for upward in range(3):
                other = (
                    ext_units[across, own_index + upward],
                    ext_values[across, own_index + upward],
                    ext_grads[across, own_index + upward],
                )
                first_force, second_force = pair_forces(
                    own, other, float(across - 1), float(upward - 1), w_filter
                )
                summed = summed + first_force
        force_rows.append(summed)
    forces = jnp.stack(force_rows)
    return forces[None]


def solution(mesh):
    placed = (
        P("plane", "tower", None, None),
        P("plane", "tower", None, None),
        P("plane", "tower", None, None),
        P(),
        P(),
        P(),
        P("plane", "tower"),
    )
    return jax.shard_map(
        on_device,
        mesh=mesh,
        in_specs=placed,
        out_specs=P("plane", "tower", None, None),
        check_vma=False,
    )
```

profile of v0, /device:TPU:4, one launch (start us, length us, event | category | flops | bytes accessed | tf_op | source)
XLA Modules:
  0.0 122.9 jit_solution(4028126179882159300)
XLA Ops:
  0.0 11.6 %collective-permute-start.1 = (bf16[1,2,3,128]{3,1,2,0:T(2,128)(2,1)}, bf16[1,2,3,128]{3,1,2,0:T(2,128)(2,1)S(1)}, u32[]{:S(2)}, u32[]{:S(2)}) collective-permute-start(bf16[1,2,3,128]{3,1,2,0:T(2,128)(2,1)} %param.7), channel_id=1, source_target_pairs={{8,0},{16,8},{24,16},{32,24},{40,32},{48,40},{56,48},{64,56},{72,6... | collective-permute-start | bytes 4616 | tf_op jit(solution)/shard_map/ppermute | solution.py:22
  11.6 1.9 %collective-permute-start = (bf16[1,2,3,128]{3,1,2,0:T(2,128)(2,1)}, bf16[1,2,3,128]{3,1,2,0:T(2,128)(2,1)S(1)}, u32[]{:S(2)}, u32[]{:S(2)}) collective-permute-start(bf16[1,2,3,128]{3,1,2,0:T(2,128)(2,1)} %param.7), channel_id=1, source_target_pairs={{0,8},{8,16},{16,24},{24,32},{32,40},{40,48},{48,56},{56,64},{64,7... | collective-permute-start | bytes 4616 | tf_op jit(solution)/shard_map/ppermute | solution.py:20
  13.6 1.2 fusion.162
  14.8 5.8 %collective-permute-start.7 = (bf16[1,2,128,256]{3,2,1,0:T(8,128)(2,1)S(1)}, bf16[1,2,128,256]{3,2,1,0:T(8,128)(2,1)S(1)}, u32[]{:S(2)}, u32[]{:S(2)}) collective-permute-start(bf16[1,2,128,256]{3,2,1,0:T(8,128)(2,1)S(1)} %bitcast.417), channel_id=1, source_target_pairs={{8,0},{16,8},{24,16},{32,24},{40,32},{48,40},{56,48},{64,56},{72,6... | collective-permute-start | bytes 393224 | tf_op jit(solution)/shard_map/ppermute | solution.py:22
  20.6 1.9 %collective-permute-start.6 = (bf16[1,2,128,256]{3,2,1,0:T(8,128)(2,1)S(1)}, bf16[1,2,128,256]{3,2,1,0:T(8,128)(2,1)S(1)}, u32[]{:S(2)}, u32[]{:S(2)}) collective-permute-start(bf16[1,2,128,256]{3,2,1,0:T(8,128)(2,1)S(1)} %bitcast.418), channel_id=1, source_target_pairs={{0,8},{8,16},{16,24},{24,32},{32,40},{40,48},{48,56},{56,64},{64,7... | collective-permute-start | bytes 393224 | tf_op jit(solution)/shard_map/ppermute | solution.py:20
  22.7 5.7 %collective-permute-start.4 = (bf16[1,2,128,256]{3,2,1,0:T(8,128)(2,1)S(1)}, bf16[1,2,128,256]{3,2,1,0:T(8,128)(2,1)S(1)}, u32[]{:S(2)}, u32[]{:S(2)}) collective-permute-start(bf16[1,2,128,256]{3,2,1,0:T(8,128)(2,1)S(1)} %bitcast.421), channel_id=1, source_target_pairs={{8,0},{16,8},{24,16},{32,24},{40,32},{48,40},{56,48},{64,56},{72,6... | collective-permute-start | bytes 393224 | tf_op jit(solution)/shard_map/ppermute | solution.py:22
  28.7 1.9 %collective-permute-start.3 = (bf16[1,2,128,256]{3,2,1,0:T(8,128)(2,1)S(1)}, bf16[1,2,128,256]{3,2,1,0:T(8,128)(2,1)S(1)}, u32[]{:S(2)}, u32[]{:S(2)}) collective-permute-start(bf16[1,2,128,256]{3,2,1,0:T(8,128)(2,1)S(1)} %bitcast.422), channel_id=1, source_target_pairs={{0,8},{8,16},{16,24},{24,32},{32,40},{40,48},{48,56},{56,64},{64,7... | collective-permute-start | bytes 393224 | tf_op jit(solution)/shard_map/ppermute | solution.py:20
  30.7 3.5 %collective-permute-start.2 = (bf16[3,1,3,128]{3,1,2,0:T(2,128)(2,1)S(1)}, bf16[3,1,3,128]{3,1,2,0:T(2,128)(2,1)S(1)}, u32[]{:S(2)}, u32[]{:S(2)}) collective-permute-start(bf16[3,1,3,128]{3,1,2,0:T(2,128)(2,1)S(1)} %get-tuple-element.116), channel_id=1, source_target_pairs={{0,1},{1,2},{2,3},{3,4},{4,5},{5,6},{6,7},{7,0},{8,9},{9,10},{10,1... | collective-permute-start | bytes 6920 | tf_op jit(solution)/shard_map/ppermute | solution.py:20
  34.9 4.9 %collective-permute-done.2 = bf16[3,1,3,128]{3,1,2,0:T(2,128)(2,1)S(1)} collective-permute-done((bf16[3,1,3,128]{3,1,2,0:T(2,128)(2,1)S(1)}, bf16[3,1,3,128]{3,1,2,0:T(2,128)(2,1)S(1)}, u32[]{:S(2)}, u32[]{:S(2)}) %collective-permute-start.2) | collective-permute-done | bytes 2336 | tf_op jit(solution)/shard_map/ppermute | solution.py:20
  39.9 1.9 %collective-permute-start.9 = (bf16[3,1,3,128]{3,1,2,0:T(2,128)(2,1)S(1)}, bf16[3,1,3,128]{3,1,2,0:T(2,128)(2,1)S(1)}, u32[]{:S(2)}, u32[]{:S(2)}) collective-permute-start(bf16[3,1,3,128]{3,1,2,0:T(2,128)(2,1)S(1)} %get-tuple-element.117), channel_id=1, source_target_pairs={{1,0},{2,1},{3,2},{4,3},{5,4},{6,5},{7,6},{0,7},{9,8},{10,9},{11,1... | collective-permute-start | bytes 6920 | tf_op jit(solution)/shard_map/ppermute | solution.py:22
  41.8 3.5 %collective-permute-done.9 = bf16[3,1,3,128]{3,1,2,0:T(2,128)(2,1)S(1)} collective-permute-done((bf16[3,1,3,128]{3,1,2,0:T(2,128)(2,1)S(1)}, bf16[3,1,3,128]{3,1,2,0:T(2,128)(2,1)S(1)}, u32[]{:S(2)}, u32[]{:S(2)}) %collective-permute-start.9) | collective-permute-done | bytes 2336 | tf_op jit(solution)/shard_map/ppermute | solution.py:22
  46.5 1.8 %multiply_add_fusion.24 = (f32[128,128]{1,0:T(8,128)S(1)}, f32[128,128]{1,0:T(8,128)S(1)}, f32[128,128]{1,0:T(8,128)S(1)}, f32[128,128]{1,0:T(8,128)S(1)}, f32[1...) fusion(f32[128]{0:T(128)S(1)} %get-tuple-element.316, ...), kind=kLoop, calls=%fused_computation.619 | loop fusion | flops 4456448 | bytes 3155456 | tf_op jit(solution)/shard_map/add | solution.py:39
  52.3 1.5 %multiply_add_fusion.22 = (f32[128,128]{1,0:T(8,128)S(1)}, f32[128,128]{1,0:T(8,128)}, f32[128,128]{1,0:T(8,128)}, f32[128,128]{1,0:T(8,128)S(1)}, f32[128,128]{...) fusion(f32[128]{0:T(128)S(1)} %get-tuple-element.290, ...), kind=kLoop, calls=%fused_computation.607 | loop fusion | flops 2785280 | bytes 1975296 | tf_op jit(solution)/shard_map/add | solution.py:39
  54.3 1.9 %collective-permute-start.8 = (bf16[3,1,128,256]{3,2,1,0:T(8,128)(2,1)S(1)}, bf16[3,1,128,256]{3,2,1,0:T(8,128)(2,1)S(1)}, u32[]{:S(2)}, u32[]{:S(2)}) collective-permute-start(bf16[3,1,128,256]{3,2,1,0:T(8,128)(2,1)S(1)} %get-tuple-element.95), channel_id=1, source_target_pairs={{0,1},{1,2},{2,3},{3,4},{4,5},{5,6},{6,7},{7,0},{8,9},{9,10},{10,1... | collective-permute-start | bytes 589832 | tf_op jit(solution)/shard_map/ppermute | solution.py:20
  56.2 7.5 %collective-permute-start.11 = (bf16[3,1,128,256]{3,2,1,0:T(8,128)(2,1)S(1)}, bf16[3,1,128,256]{3,2,1,0:T(8,128)(2,1)S(1)}, u32[]{:S(2)}, u32[]{:S(2)}) collective-permute-start(bf16[3,1,128,256]{3,2,1,0:T(8,128)(2,1)S(1)} %get-tuple-element.96), channel_id=1, source_target_pairs={{1,0},{2,1},{3,2},{4,3},{5,4},{6,5},{7,6},{0,7},{9,8},{10,9},{11,1... | collective-permute-start | bytes 589832 | tf_op jit(solution)/shard_map/ppermute | solution.py:22
  63.8 1.9 %collective-permute-start.5 = (bf16[3,1,128,256]{3,2,1,0:T(8,128)(2,1)S(1)}, bf16[3,1,128,256]{3,2,1,0:T(8,128)(2,1)}, u32[]{:S(2)}, u32[]{:S(2)}) collective-permute-start(bf16[3,1,128,256]{3,2,1,0:T(8,128)(2,1)S(1)} %get-tuple-element.97), channel_id=1, source_target_pairs={{0,1},{1,2},{2,3},{3,4},{4,5},{5,6},{6,7},{7,0},{8,9},{9,10},{10,1... | collective-permute-start | bytes 589832 | tf_op jit(solution)/shard_map/ppermute | solution.py:20
  65.8 7.7 %collective-permute-start.10 = (bf16[3,1,128,256]{3,2,1,0:T(8,128)(2,1)S(1)}, bf16[3,1,128,256]{3,2,1,0:T(8,128)(2,1)}, u32[]{:S(2)}, u32[]{:S(2)}) collective-permute-start(bf16[3,1,128,256]{3,2,1,0:T(8,128)(2,1)S(1)} %get-tuple-element.98), channel_id=1, source_target_pairs={{1,0},{2,1},{3,2},{4,3},{5,4},{6,5},{7,6},{0,7},{9,8},{10,9},{11,1... | collective-permute-start | bytes 589832 | tf_op jit(solution)/shard_map/ppermute | solution.py:22
  79.3 1.8 %fusion.91 = f32[128,128]{1,0:T(8,128)} fusion(bf16[128,256]{1,0:T(8,128)(2,1)} %get-tuple-element.112, f32[128,128]{1,0:T(8,128)S(1)} %copy-done.35, f32[128,128]{1,0:T(8,128)S(1)} %copy-done.36, f32[128,128]{1,0:T(8,128)} %get-tuple-element.238, bf16[8,256]{1,0:T(8,128)(2,1)S(1)} %copy-done.180, f32[8]{0:T(128)S(1)} %copy-done.189, ...), kind=kOutput, calls=%fused_computation.73 | convolution fusion | flops 68403200 | bytes 397824 | tf_op jit(solution)/shard_map/dot_general | solution.py:53
  82.8 1.9 %fusion.105 = f32[128,128]{1,0:T(8,128)} fusion(f32[128,128]{1,0:T(8,128)S(1)} %copy-done.49, f32[128,128]{1,0:T(8,128)} %get-tuple-element.340, f32[128,128]{1,0:T(8,128)} %get-tuple-element.341, bf16[128,256]{1,0:T(8,128)(2,1)} %get-tuple-element.109, bf16[8,256]{1,0:T(8,128)(2,1)S(1)} %copy-done.181, f32[8]{0:T(128)S(1)} %copy-done.190, ...), kind=kOutput, calls=%fused_computation.87 | convolution fusion | flops 68403200 | bytes 397824 | tf_op jit(solution)/shard_map/dot_general | solution.py:53
  97.4 1.8 %fusion.129 = f32[128,128]{1,0:T(8,128)} fusion(f32[128,128]{1,0:T(8,128)S(1)} %copy-done.9, f32[128,128]{1,0:T(8,128)} %get-tuple-element.241, f32[128,128]{1,0:T(8,128)S(1)} %copy-done.8, bf16[128,256]{1,0:T(8,128)(2,1)} %copy-done.60, bf16[8,256]{1,0:T(8,128)(2,1)S(1)} %copy-done.182, f32[8]{0:T(128)S(1)} %copy-done.191, ...), kind=kOutput, calls=%fused_computation.97 | convolution fusion | flops 68403200 | bytes 397824 | tf_op jit(solution)/shard_map/dot_general | solution.py:48
  101.4 1.2 fusion.117
  110.0 1.2 fusion.141
  115.4 1.2 fusion.108
  119.1 1.2 fusion.159
  (487 shorter events, 43.8 us)
Async XLA Ops:
  0.0 28.7 %collective-permute-start.1 = (bf16[1,2,3,128]{3,1,2,0:T(2,128)(2,1)}, bf16[1,2,3,128]{3,1,2,0:T(2,128)(2,1)S(1)}, u32[]{:S(2)}, u32[]{:S(2)}) collective-permute-start(bf16[1,2,3,128]{3,1,2,0:T(2,128)(2,1)} %param.7), channel_id=1, source_target_pairs={{8,0},{16,8},{24,16},{32,24},{40,32},{48,40},{56,48},{64,56},{72,6... | collective-permute-start | bytes 4616 | tf_op jit(solution)/shard_map/ppermute | solution.py:22
  11.6 19.1 %collective-permute-start = (bf16[1,2,3,128]{3,1,2,0:T(2,128)(2,1)}, bf16[1,2,3,128]{3,1,2,0:T(2,128)(2,1)S(1)}, u32[]{:S(2)}, u32[]{:S(2)}) collective-permute-start(bf16[1,2,3,128]{3,1,2,0:T(2,128)(2,1)} %param.7), channel_id=1, source_target_pairs={{0,8},{8,16},{16,24},{24,32},{32,40},{40,48},{48,56},{56,64},{64,7... | collective-permute-start | bytes 4616 | tf_op jit(solution)/shard_map/ppermute | solution.py:20
  14.8 39.3 %collective-permute-start.7 = (bf16[1,2,128,256]{3,2,1,0:T(8,128)(2,1)S(1)}, bf16[1,2,128,256]{3,2,1,0:T(8,128)(2,1)S(1)}, u32[]{:S(2)}, u32[]{:S(2)}) collective-permute-start(bf16[1,2,128,256]{3,2,1,0:T(8,128)(2,1)S(1)} %bitcast.417), channel_id=1, source_target_pairs={{8,0},{16,8},{24,16},{32,24},{40,32},{48,40},{56,48},{64,56},{72,6... | collective-permute-start | bytes 393224 | tf_op jit(solution)/shard_map/ppermute | solution.py:22
  20.6 33.6 %collective-permute-start.6 = (bf16[1,2,128,256]{3,2,1,0:T(8,128)(2,1)S(1)}, bf16[1,2,128,256]{3,2,1,0:T(8,128)(2,1)S(1)}, u32[]{:S(2)}, u32[]{:S(2)}) collective-permute-start(bf16[1,2,128,256]{3,2,1,0:T(8,128)(2,1)S(1)} %bitcast.418), channel_id=1, source_target_pairs={{0,8},{8,16},{16,24},{24,32},{32,40},{40,48},{48,56},{56,64},{64,7... | collective-permute-start | bytes 393224 | tf_op jit(solution)/shard_map/ppermute | solution.py:20
  22.7 41.0 %collective-permute-start.4 = (bf16[1,2,128,256]{3,2,1,0:T(8,128)(2,1)S(1)}, bf16[1,2,128,256]{3,2,1,0:T(8,128)(2,1)S(1)}, u32[]{:S(2)}, u32[]{:S(2)}) collective-permute-start(bf16[1,2,128,256]{3,2,1,0:T(8,128)(2,1)S(1)} %bitcast.421), channel_id=1, source_target_pairs={{8,0},{16,8},{24,16},{32,24},{40,32},{48,40},{56,48},{64,56},{72,6... | collective-permute-start | bytes 393224 | tf_op jit(solution)/shard_map/ppermute | solution.py:22
  28.5 19.8 %copy-start.63 = (bf16[128,256]{1,0:T(8,128)(2,1)}, bf16[128,256]{1,0:T(8,128)(2,1)S(1)}, u32[]{:S(2)}) copy-start(bf16[128,256]{1,0:T(8,128)(2,1)S(1)} %get-tuple-element.107) | copy-start | bytes 196612
  28.6 22.1 %copy-start.60 = (bf16[128,256]{1,0:T(8,128)(2,1)}, bf16[128,256]{1,0:T(8,128)(2,1)S(1)}, u32[]{:S(2)}) copy-start(bf16[128,256]{1,0:T(8,128)(2,1)S(1)} %get-tuple-element.106) | copy-start | bytes 196612
  28.6 25.2 %copy-start.57 = (bf16[128,256]{1,0:T(8,128)(2,1)}, bf16[128,256]{1,0:T(8,128)(2,1)S(1)}, u32[]{:S(2)}) copy-start(bf16[128,256]{1,0:T(8,128)(2,1)S(1)} %get-tuple-element.105) | copy-start | bytes 196612
  28.6 17.4 %copy-start.120 = (f32[128]{0:T(128)}, f32[128]{0:T(128)S(1)}, u32[]{:S(2)}) copy-start(f32[128]{0:T(128)S(1)} %get-tuple-element.319) | copy-start | bytes 1540
  28.6 23.5 %copy-start.73 = (f32[128]{0:T(128)}, f32[128]{0:T(128)S(1)}, u32[]{:S(2)}) copy-start(f32[128]{0:T(128)S(1)} %get-tuple-element.320) | copy-start | bytes 1540
  28.6 23.5 %copy-start.76 = (f32[128]{0:T(128)}, f32[128]{0:T(128)S(1)}, u32[]{:S(2)}) copy-start(f32[128]{0:T(128)S(1)} %get-tuple-element.321) | copy-start | bytes 1540
  28.6 17.3 %copy-start.122 = (f32[128]{0:T(128)}, f32[128]{0:T(128)S(1)}, u32[]{:S(2)}) copy-start(f32[128]{0:T(128)S(1)} %get-tuple-element.314) | copy-start | bytes 1540
  28.7 25.1 %copy-start.186 = (f32[8]{0:T(128)}, f32[8]{0:T(128)S(1)}, u32[]{:S(2)}) copy-start(f32[8]{0:T(128)S(1)} %convert_multiply_fusion) | copy-start | bytes 100
  28.7 35.1 %collective-permute-start.3 = (bf16[1,2,128,256]{3,2,1,0:T(8,128)(2,1)S(1)}, bf16[1,2,128,256]{3,2,1,0:T(8,128)(2,1)S(1)}, u32[]{:S(2)}, u32[]{:S(2)}) collective-permute-start(bf16[1,2,128,256]{3,2,1,0:T(8,128)(2,1)S(1)} %bitcast.422), channel_id=1, source_target_pairs={{0,8},{8,16},{16,24},{24,32},{32,40},{40,48},{48,56},{56,64},{64,7... | collective-permute-start | bytes 393224 | tf_op jit(solution)/shard_map/ppermute | solution.py:20
  30.6 20.3 %copy-start.124 = (f32[128]{0:T(128)}, f32[128]{0:T(128)S(1)}, u32[]{:S(2)}) copy-start(f32[128]{0:T(128)S(1)} %get-tuple-element.296) | copy-start | bytes 1540
  30.6 21.5 %copy-start.79 = (f32[128]{0:T(128)}, f32[128]{0:T(128)S(1)}, u32[]{:S(2)}) copy-start(f32[128]{0:T(128)S(1)} %get-tuple-element.297) | copy-start | bytes 1540
  30.6 21.5 %copy-start.82 = (f32[128]{0:T(128)}, f32[128]{0:T(128)S(1)}, u32[]{:S(2)}) copy-start(f32[128]{0:T(128)S(1)} %get-tuple-element.298) | copy-start | bytes 1540
  30.7 21.5 %copy-start.134 = (f32[128]{0:T(128)}, f32[128]{0:T(128)S(1)}, u32[]{:S(2)}) copy-start(f32[128]{0:T(128)S(1)} %get-tuple-element.295) | copy-start | bytes 1540
  30.7 9.1 %collective-permute-start.2 = (bf16[3,1,3,128]{3,1,2,0:T(2,128)(2,1)S(1)}, bf16[3,1,3,128]{3,1,2,0:T(2,128)(2,1)S(1)}, u32[]{:S(2)}, u32[]{:S(2)}) collective-permute-start(bf16[3,1,3,128]{3,1,2,0:T(2,128)(2,1)S(1)} %get-tuple-element.116), channel_id=1, source_target_pairs={{0,1},{1,2},{2,3},{3,4},{4,5},{5,6},{6,7},{7,0},{8,9},{9,10},{10,1... | collective-permute-start | bytes 6920 | tf_op jit(solution)/shard_map/ppermute | solution.py:20
  39.9 5.5 %collective-permute-start.9 = (bf16[3,1,3,128]{3,1,2,0:T(2,128)(2,1)S(1)}, bf16[3,1,3,128]{3,1,2,0:T(2,128)(2,1)S(1)}, u32[]{:S(2)}, u32[]{:S(2)}) collective-permute-start(bf16[3,1,3,128]{3,1,2,0:T(2,128)(2,1)S(1)} %get-tuple-element.117), channel_id=1, source_target_pairs={{1,0},{2,1},{3,2},{4,3},{5,4},{6,5},{7,6},{0,7},{9,8},{10,9},{11,1... | collective-permute-start | bytes 6920 | tf_op jit(solution)/shard_map/ppermute | solution.py:22
  54.3 51.3 %collective-permute-start.8 = (bf16[3,1,128,256]{3,2,1,0:T(8,128)(2,1)S(1)}, bf16[3,1,128,256]{3,2,1,0:T(8,128)(2,1)S(1)}, u32[]{:S(2)}, u32[]{:S(2)}) collective-permute-start(bf16[3,1,128,256]{3,2,1,0:T(8,128)(2,1)S(1)} %get-tuple-element.95), channel_id=1, source_target_pairs={{0,1},{1,2},{2,3},{3,4},{4,5},{5,6},{6,7},{7,0},{8,9},{9,10},{10,1... | collective-permute-start | bytes 589832 | tf_op jit(solution)/shard_map/ppermute | solution.py:20
  56.2 43.1 %collective-permute-start.11 = (bf16[3,1,128,256]{3,2,1,0:T(8,128)(2,1)S(1)}, bf16[3,1,128,256]{3,2,1,0:T(8,128)(2,1)S(1)}, u32[]{:S(2)}, u32[]{:S(2)}) collective-permute-start(bf16[3,1,128,256]{3,2,1,0:T(8,128)(2,1)S(1)} %get-tuple-element.96), channel_id=1, source_target_pairs={{1,0},{2,1},{3,2},{4,3},{5,4},{6,5},{7,6},{0,7},{9,8},{10,9},{11,1... | collective-permute-start | bytes 589832 | tf_op jit(solution)/shard_map/ppermute | solution.py:22
  63.8 45.4 %collective-permute-start.5 = (bf16[3,1,128,256]{3,2,1,0:T(8,128)(2,1)S(1)}, bf16[3,1,128,256]{3,2,1,0:T(8,128)(2,1)}, u32[]{:S(2)}, u32[]{:S(2)}) collective-permute-start(bf16[3,1,128,256]{3,2,1,0:T(8,128)(2,1)S(1)} %get-tuple-element.97), channel_id=1, source_target_pairs={{0,1},{1,2},{2,3},{3,4},{4,5},{5,6},{6,7},{7,0},{8,9},{9,10},{10,1... | collective-permute-start | bytes 589832 | tf_op jit(solution)/shard_map/ppermute | solution.py:20
  65.8 34.9 %collective-permute-start.10 = (bf16[3,1,128,256]{3,2,1,0:T(8,128)(2,1)S(1)}, bf16[3,1,128,256]{3,2,1,0:T(8,128)(2,1)}, u32[]{:S(2)}, u32[]{:S(2)}) collective-permute-start(bf16[3,1,128,256]{3,2,1,0:T(8,128)(2,1)S(1)} %get-tuple-element.98), channel_id=1, source_target_pairs={{1,0},{2,1},{3,2},{4,3},{5,4},{6,5},{7,6},{0,7},{9,8},{10,9},{11,1... | collective-permute-start | bytes 589832 | tf_op jit(solution)/shard_map/ppermute | solution.py:22
  (182 other events, 403.3 us)
where the time goes:
time: 125 us; the launch traced here: 123 us
  starting transfers between devices  53.3 us (43%)
  matrix products  26.8 us (21%)
  local copies, waits for them, and re-layouts  22.3 us (18%)
  other arithmetic  9.3 us (7%)
  waiting for transfers between devices  8.47 us (7%)
  between operations  2.64 us (2%)
    ppermute x6, starting transfers between devices, extended(): lax.ppermute(head, axis, [((i + 1) % count, i) for i in range(count)])  40.3 us
    unnamed x390, local copies, waits for them, and re-layouts  15.5 us
    dot_general x18, matrix products, pair_forces(): lax.dot_general(filtered, second[1], (((1,), (1,)), ((), ())), preferred_...  14.2 us
    ppermute x6, starting transfers between devices, extended(): lax.ppermute(tail, axis, [(i, (i + 1) % count) for i in range(count)])  13.1 us
    dot_general x18, matrix products, pair_forces(): lax.dot_general(filtered_back, first[1], (((1,), (1,)), ((), ())), prefer...  11.3 us
    ppermute x6, waiting for transfers between devices, extended(): lax.ppermute(tail, axis, [(i, (i + 1) % count) for i in range(count)])  4.93 us
    add x3, other arithmetic, pair_forces(): squared = along_x * along_x + along_y * along_y + along_z * along_z  4.42 us
    reduce_sum x18, local copies, waits for them, and re-layouts, pair_forces(): jnp.sum(slopes_back * backward.reshape(atoms, radial, atoms), axis=1)  4.21 us
  transfers between devices with their start and end apart: 12, of which 2 were waited for; matrix products, arithmetic and copies ran while one was open for 27% of the time, Pallas kernels for 0%

commit v1 on v0

v1 whole, which is shorter than its diff:
```python
import math

import jax
import jax.numpy as jnp
from jax import lax
from jax.experimental import pallas as pl
from jax.experimental.pallas import tpu as pltpu
from jax.sharding import PartitionSpec as P

PITCH = 12.5
CUTOFF_SQUARED = 25.0
CENTER_STEP = 3.125
GAMMA = 0.2
FORCE_UNIT = 0.005
LOG2E = math.log2(math.e)

BOX = 128
F = 256
RADIAL = 8
MIDDLE = 4
ROWS = 16

STEPS = [math.exp(-GAMMA * CENTER_STEP**2 * (2 * m - 1)) for m in range(1, MIDDLE + 1)]


def vmem():
    return pl.BlockSpec(memory_space=pltpu.VMEM)


def smem():
    return pl.BlockSpec(memory_space=pltpu.SMEM)


def params(mib):
    return pltpu.CompilerParams(vmem_limit_bytes=mib * 2**20)


def packed_offsets(rows):
    tall = jnp.concatenate([rows, jnp.zeros((16 - rows.shape[0], BOX), jnp.float32)], axis=0)
    wide = jnp.concatenate([tall, jnp.zeros((16, 2 * F - BOX), jnp.float32)], axis=1)
    return wide.astype(jnp.bfloat16)


def prepare(odd_ref, counts_ref, offsets_ref, features_ref, cotangent_ref, w_in_ref, w_out_ref, own_ref, first_ref, second_ref):
    odd = odd_ref[0] == 1
    slots = lax.broadcasted_iota(jnp.int32, (BOX, F), 0)
    offsets = offsets_ref[...].astype(jnp.float32)
    boxes = []
    for b in range(2):
        live = slots < counts_ref[0, b]
        values = jnp.dot(features_ref[b], w_in_ref[...], preferred_element_type=jnp.float32)
        grads = lax.dot_general(
            cotangent_ref[b], w_out_ref[...], (((1,), (1,)), ((), ())), preferred_element_type=jnp.float32
        )
        both = jnp.concatenate([jnp.where(live, values, 0.0), jnp.where(live, grads, 0.0)], axis=1)
        boxes.append(both)
        own_ref[b * BOX : (b + 1) * BOX, :] = both.astype(jnp.bfloat16)
    own_ref[2 * BOX :, :] = packed_offsets(offsets.reshape(6, BOX))
    first_ref[:BOX, :] = jnp.where(odd, boxes[0], boxes[1]).astype(jnp.bfloat16)
    second_ref[:BOX, :] = jnp.where(odd, boxes[1], boxes[0]).astype(jnp.bfloat16)
    first_ref[BOX:, :] = packed_offsets(jnp.where(odd, offsets[:, 0], offsets[:, 1]))
    second_ref[BOX:, :] = packed_offsets(jnp.where(odd, offsets[:, 1], offsets[:, 0]))


def join(odd_ref, own_ref, first_ref, second_ref, column_ref):
    odd = odd_ref[0] == 1
    first = first_ref[...].astype(jnp.float32)
    second = second_ref[...].astype(jnp.float32)
    below = jnp.where(odd, first, second)
    above = jnp.where(odd, second, first)
    column_ref[:BOX, :] = below[:BOX].astype(jnp.bfloat16)
    column_ref[BOX : 3 * BOX, :] = own_ref[: 2 * BOX, :]
    column_ref[3 * BOX : 4 * BOX, :] = above[:BOX].astype(jnp.bfloat16)
    own = own_ref[2 * BOX :, :BOX].astype(jnp.float32)
    rows = []
    for c in range(3):
        rows += [below[BOX + c : BOX + c + 1, :BOX], own[2 * c : 2 * c + 2], above[BOX + c : BOX + c + 1, :BOX]]
    column_ref[4 * BOX :, :] = packed_offsets(jnp.concatenate(rows, axis=0))


def spread_weights(own_ref, w_filter_ref, out_ref):
    for b in range(2):
        values = own_ref[b * BOX : (b + 1) * BOX, :F].astype(jnp.float32)
        grads = own_ref[b * BOX : (b + 1) * BOX, F:].astype(jnp.float32)
        for k in range(RADIAL):
            w = w_filter_ref[k : k + 1, :].astype(jnp.float32)
            out_ref[b, k * BOX : (k + 1) * BOX, :F] = (grads * w).astype(jnp.bfloat16)
            out_ref[b, k * BOX : (k + 1) * BOX, F:] = (values * w).astype(jnp.bfloat16)


def strengths(dx, dy, dz, amplitudes):
    q = dx * dx + dy * dy + dz * dz
    c = jnp.maximum(1.0 - q * (1.0 / CUTOFF_SQUARED), 0.0)
    h = jnp.minimum(q, CUTOFF_SQUARED) - MIDDLE * CENTER_STEP
    middle = jnp.exp2(h * h * (-GAMMA * LOG2E))
    slope = 2.0 * GAMMA * CENTER_STEP * LOG2E
    up = jnp.exp2(h * slope)
    down = jnp.exp2(h * -slope)
    step = up * STEPS[2]
    p = step * amplitudes[7]
    d = p
    p = amplitudes[6] + p
    for m in (1, 0):
        step = up * STEPS[m]
        p = step * p
        d = step * d + p
        p = amplitudes[MIDDLE + m] + p
    step = down * STEPS[3]
    s = step * amplitudes[0]
    e = s
    s = amplitudes[1] + s
    for m in (2, 1):
        step = down * STEPS[m]
        s = step * s
        e = step * e + s
        s = amplitudes[MIDDLE - m] + s
    step = down * STEPS[0]
    s = step * s
    e = step * e + s
    p = p + s
    d = d - e
    hc = h * c
    inner = (hc * (-2.0 * GAMMA) - 2.0 / CUTOFF_SQUARED) * p + (c * (2.0 * GAMMA * CENTER_STEP)) * d
    return (middle * c) * inner


def pairs(shift_ref, own_ref, weights_ref, column_ref, before_ref, forces_ref):
    own = own_ref[2 * BOX :, :BOX].astype(jnp.float32) * PITCH
    theirs = column_ref[4 * BOX :, :BOX].astype(jnp.float32) * PITCH
    theirs = jnp.transpose(jnp.concatenate([theirs, jnp.zeros((BOX - 16, BOX), jnp.float32)], axis=0))
    across = shift_ref[0] * PITCH
    results = [[None, None] for _ in range(3)]
    for b in range(2):
        mine = [own[2 * c + b : 2 * c + b + 1] for c in range(3)]
        totals = [jnp.zeros((ROWS, BOX), jnp.float32) for _ in range(3)]
        for upward in range(3):
            s = b + upward
            product = lax.dot_general(
                column_ref[s * BOX : (s + 1) * BOX, :],
                weights_ref[b],
                (((1,), (1,)), ((), ())),
                preferred_element_type=jnp.float32,
            )
            shifts = [across, (upward - 1) * PITCH, 0.0]
            for r in range(0, BOX, ROWS):
                along = [
                    (theirs[r : r + ROWS, 4 * c + s : 4 * c + s + 1] + shifts[c]) - mine[c] for c in range(3)
                ]
                strength = strengths(
                    *along, [product[r : r + ROWS, k * BOX : (k + 1) * BOX] for k in range(RADIAL)]
                )
                totals = [t + strength * a for t, a in zip(totals, along, strict=True)]
        for c in range(3):
            results[c][b] = jnp.sum(totals[c], axis=0, keepdims=True) * (2.0 * FORCE_UNIT)
    for c in range(3):
        forces_ref[c] = before_ref[c] + jnp.concatenate(results[c], axis=0)


def swap(x, axis, later):
    n = lax.axis_size(axis)
    if later:
        perm = [(i, (i + 1) % n if i % 2 else (i - 1) % n) for i in range(n)]
    else:
        perm = [(i, i + 1 - 2 * (i % 2)) for i in range(n)]
    return lax.ppermute(x, axis, perm)


def on_device(offsets, features, cotangent, w_in, w_out, w_filter, counts):
    bf16 = jnp.bfloat16
    odd = (lax.axis_index("tower") % 2).astype(jnp.int32)[None]
    side = 1.0 - 2.0 * (lax.axis_index("plane") % 2).astype(jnp.float32)[None]
    turned = jnp.transpose(offsets[0], (1, 0, 2))
    own, first, second = pl.pallas_call(
        prepare,
        out_shape=(
            jax.ShapeDtypeStruct((2 * BOX + 16, 2 * F), bf16),
            jax.ShapeDtypeStruct((BOX + 16, 2 * F), bf16),
            jax.ShapeDtypeStruct((BOX + 16, 2 * F), bf16),
        ),
        in_specs=[smem(), smem()] + [vmem()] * 5,
        out_specs=(vmem(),) * 3,
        compiler_params=params(16),
        name="prepare",
    )(odd, counts, turned, features[0], cotangent[0], w_in, w_out)
    second = swap(second, "tower", True)
    first = swap(first, "tower", False)
    weights = pl.pallas_call(
        spread_weights,
        out_shape=jax.ShapeDtypeStruct((2, RADIAL * BOX, 2 * F), bf16),
        in_specs=[vmem()] * 2,
        out_specs=vmem(),
        compiler_params=params(16),
        name="spread_weights",
    )(own, w_filter)
    column = pl.pallas_call(
        join,
        out_shape=jax.ShapeDtypeStruct((4 * BOX + 16, 2 * F), bf16),
        in_specs=[smem()] + [vmem()] * 3,
        out_specs=vmem(),
        compiler_params=params(16),
        name="join",
    )(odd, own, first, second)
    outer = swap(column, "plane", True)
    inner = swap(column, "plane", False)
    forces = jnp.zeros((3, 2, BOX), jnp.float32)
    for name, shift, source in (("same", side * 0.0, column), ("inner", side, inner), ("outer", -side, outer)):
        forces = pl.pallas_call(
            pairs,
            out_shape=jax.ShapeDtypeStruct((3, 2, BOX), jnp.float32),
            in_specs=[smem()] + [vmem()] * 4,
            out_specs=vmem(),
            compiler_params=params(32),
            cost_estimate=pl.CostEstimate(flops=6 * 2**27, bytes_accessed=2**21, transcendentals=0),
            name="pairs_" + name,
        )(shift, own, weights, source, forces)
    return jnp.transpose(forces, (1, 0, 2))[None]


def solution(mesh):
    placed = (
        P("plane", "tower", None, None),
        P("plane", "tower", None, None),
        P("plane", "tower", None, None),
        P(),
        P(),
        P(),
        P("plane", "tower"),
    )
    return jax.shard_map(
        on_device,
        mesh=mesh,
        in_specs=placed,
        out_specs=P("plane", "tower", None, None),
        check_vma=False,
    )
```

time: 125 us -> 47 us (0.38)
  the two profiles are of different devices: /device:TPU:4 before, /device:TPU:1 now
where the time goes in v1:
time: 47 us; the launch traced here: 46.7 us
  starting transfers between devices  20.1 us (43%)
  waiting for transfers between devices  11 us (23%)
  Pallas kernels  9.89 us (21%)
  local copies, waits for them, and re-layouts  5.63 us (12%)
    ppermute x4, starting transfers between devices, swap(): return lax.ppermute(x, axis, perm)  20.1 us
    ppermute x4, waiting for transfers between devices, swap(): return lax.ppermute(x, axis, perm)  11 us
    pallas_call x3, Pallas kernels, on_device(): pl.pallas_call(pairs, out_shape=jax.ShapeDtypeStruct((3, 2, BOX), jnp.flo...  8.75 us
    unnamed x14, local copies, waits for them, and re-layouts  5.63 us
  transfers between devices with their start and end apart: 4, of which 2 were waited for; matrix products, arithmetic and copies ran while one was open for 0% of the time, Pallas kernels for 13%

profile of v1, /device:TPU:1, one launch (start us, length us, event | category | flops | bytes accessed | tf_op | source)
XLA Modules:
  0.0 46.7 jit_solution(13628952825962167442)
XLA Ops:
  0.0 0.0 copy-start
  0.0 0.9 %copy-done = bf16[1,2,128,256]{3,2,1,0:T(8,128)(2,1)S(1)} copy-done((bf16[1,2,128,256]{3,2,1,0:T(8,128)(2,1)S(1)}, bf16[1,2,128,256]{3,2,1,0:T(8,128)(2,1)}, u32[]{:S(2)}) %copy-start) | copy-done | bytes 131096
  0.9 0.0 copy-start.1
  0.9 0.9 %copy-done.1 = bf16[1,2,128,256]{3,2,1,0:T(8,128)(2,1)S(1)} copy-done((bf16[1,2,128,256]{3,2,1,0:T(8,128)(2,1)S(1)}, bf16[1,2,128,256]{3,2,1,0:T(8,128)(2,1)}, u32[]{:S(2)}) %copy-start.1) | copy-done | bytes 131096
  1.8 0.9 %copy-done.2 = bf16[256,256]{1,0:T(8,128)(2,1)S(1)} copy-done((bf16[256,256]{1,0:T(8,128)(2,1)S(1)}, bf16[256,256]{1,0:T(8,128)(2,1)}, u32[]{:S(2)}) %copy-start.2) | copy-done | bytes 131096
  2.7 0.9 %copy-done.3 = bf16[256,256]{1,0:T(8,128)(2,1)S(1)} copy-done((bf16[256,256]{1,0:T(8,128)(2,1)S(1)}, bf16[256,256]{1,0:T(8,128)(2,1)}, u32[]{:S(2)}) %copy-start.3) | copy-done | bytes 131096
  3.6 0.7 %copy-done.5 = bf16[1,2,3,128]{3,1,2,0:T(2,128)(2,1)S(1)} copy-done((bf16[1,2,3,128]{3,1,2,0:T(2,128)(2,1)S(1)}, bf16[1,2,3,128]{3,1,2,0:T(2,128)(2,1)}, u32[]{:S(2)}) %copy-start.5) | copy-done | bytes 1560
  4.3 0.7 %copy-done.6 = s32[1,2]{1,0:T(1,128)S(1)} copy-done((s32[1,2]{1,0:T(1,128)S(1)}, s32[1,2]{1,0:T(1,128)}, u32[]{:S(2)}) %copy-start.6) | copy-done | bytes 32
  5.0 0.8 %prepare.1 = (bf16[272,512]{1,0:T(8,128)(2,1)S(1)}, bf16[144,512]{1,0:T(8,128)(2,1)S(1)}, bf16[144,512]{1,0:T(8,128)(2,1)S(1)}) custom-call(s32[1]{0:T(128)} %bitcast.1.odd_ref, s32[1,2]{1,0:T(1,128)S(1)} %copy-done.6, bf16[3,2,128]{2,1,0:T(2,128)(2,1)S(1)} %bitcast.12, bf16[2,128,256]{2,1,0:T(8,128)(2,1)S(1)} %bitcast.10, ...), custom_call_target="tpu_custom_call" | custom-call | tf_op jit(solution)/shard_map/prepare/pallas_call | solution.py:173
  5.8 4.0 %collective-permute-start = (bf16[144,512]{1,0:T(8,128)(2,1)S(1)}, bf16[144,512]{1,0:T(8,128)(2,1)S(1)}, u32[]{:S(2)}, u32[]{:S(2)}) collective-permute-start(bf16[144,512]{1,0:T(8,128)(2,1)S(1)} %get-tuple-element.9), channel_id=1, source_target_pairs={{0,1},{1,0},{2,3},{3,2},{4,5},{5,4},{6,7},{7,6},{8,9},{9,8},{10,11... | collective-permute-start | bytes 442376 | tf_op jit(solution)/shard_map/ppermute | solution.py:165
  9.8 6.3 %collective-permute-start.1 = (bf16[144,512]{1,0:T(8,128)(2,1)S(1)}, bf16[144,512]{1,0:T(8,128)(2,1)S(1)}, u32[]{:S(2)}, u32[]{:S(2)}) collective-permute-start(bf16[144,512]{1,0:T(8,128)(2,1)S(1)} %get-tuple-element.10), channel_id=1, source_target_pairs={{0,7},{1,2},{2,1},{3,4},{4,3},{5,6},{6,5},{7,0},{8,15},{9,10},{10,... | collective-permute-start | bytes 442376 | tf_op jit(solution)/shard_map/ppermute | solution.py:165
  16.1 0.0 collective-permute-done.first_ref
  16.1 3.2 %collective-permute-done.1.second_ref = bf16[144,512]{1,0:T(8,128)(2,1)S(1)} collective-permute-done((bf16[144,512]{1,0:T(8,128)(2,1)S(1)}, bf16[144,512]{1,0:T(8,128)(2,1)S(1)}, u32[]{:S(2)}, u32[]{:S(2)}) %collective-permute-start.1) | collective-permute-done | bytes 147488 | tf_op jit(solution)/shard_map/ppermute | solution.py:165
  19.3 0.1 join.1.column_ref
  19.4 7.8 %collective-permute-start.3 = (bf16[528,512]{1,0:T(8,128)(2,1)S(1)}, bf16[528,512]{1,0:T(8,128)(2,1)}, u32[]{:S(2)}, u32[]{:S(2)}) collective-permute-start(bf16[528,512]{1,0:T(8,128)(2,1)S(1)} %join.1.column_ref), channel_id=1, source_target_pairs={{0,8},{8,0},{16,24},{24,16},{32,40},{40,32},{48,56},{56,48},{64,72... | collective-permute-start | bytes 1622024 | tf_op jit(solution)/shard_map/ppermute | solution.py:165
  27.2 1.9 %collective-permute-start.2 = (bf16[528,512]{1,0:T(8,128)(2,1)S(1)}, bf16[528,512]{1,0:T(8,128)(2,1)S(1)}, u32[]{:S(2)}, u32[]{:S(2)}) collective-permute-start(bf16[528,512]{1,0:T(8,128)(2,1)S(1)} %join.1.column_ref), channel_id=1, source_target_pairs={{0,504},{8,16},{16,8},{24,32},{32,24},{40,48},{48,40},{56,64},{64,... | collective-permute-start | bytes 1622024 | tf_op jit(solution)/shard_map/ppermute | solution.py:165
  29.2 0.0 copy-start.4
  29.2 0.7 %copy-done.4 = bf16[8,256]{1,0:T(8,128)(2,1)S(1)} copy-done((bf16[8,256]{1,0:T(8,128)(2,1)S(1)}, bf16[8,256]{1,0:T(8,128)(2,1)}, u32[]{:S(2)}) %copy-start.4) | copy-done | bytes 4120
  29.9 0.3 spread_weights.1.weights_ref
  30.1 2.4 %pairs_same.1.before_ref = f32[3,2,128]{2,1,0:T(2,128)S(1)} custom-call(f32[1]{0:T(128)S(6)} %mul.8.shift_ref, bf16[272,512]{1,0:T(8,128)(2,1)S(1)} %get-tuple-element.8.own_ref, bf16[2,1024,512]{2,1,0:T(8,128)(2,1)S(1)} %spread_weights.1.weights_ref, bf16[528,512]{1,0:T(8,128)(2,1)S(1)} %join.1.column_ref, f32[3,2,128]{2,1,0:T(2,128)S(1)} %broadcast_in_dim.11.before_ref), custom_call_target="tpu_custom_call" | custom-call | flops 805306368 | bytes 2097152 | tf_op jit(solution)/shard_map/pairs_same/pallas_call | solution.py:207
  32.5 0.0 collective-permute-done.3.column_ref
  32.5 3.4 %pairs_inner.1.before_ref = f32[3,2,128]{2,1,0:T(2,128)S(1)} custom-call(f32[1]{0:T(128)} %bitcast.shift_ref, bf16[272,512]{1,0:T(8,128)(2,1)S(1)} %get-tuple-element.8.own_ref, bf16[2,1024,512]{2,1,0:T(8,128)(2,1)S(1)} %spread_weights.1.weights_ref, bf16[528,512]{1,0:T(8,128)(2,1)} %collective-permute-done.3.column_ref, f32[3,2,128]{2,1,0:T(2,128)S(1)} %pairs_same.1.before_ref), custom_call_target="tpu_custom_call" | custom-call | flops 805306368 | bytes 2097152 | tf_op jit(solution)/shard_map/pairs_inner/pallas_call | solution.py:207
  36.0 7.7 %collective-permute-done.2.column_ref = bf16[528,512]{1,0:T(8,128)(2,1)S(1)} collective-permute-done((bf16[528,512]{1,0:T(8,128)(2,1)S(1)}, bf16[528,512]{1,0:T(8,128)(2,1)S(1)}, u32[]{:S(2)}, u32[]{:S(2)}) %collective-permute-start.2) | collective-permute-done | bytes 540704 | tf_op jit(solution)/shard_map/ppermute | solution.py:165
  43.7 2.9 %pairs_outer.1 = f32[3,2,128]{2,1,0:T(2,128)} custom-call(f32[1]{0:T(128)S(6)} %neg.3.shift_ref, bf16[272,512]{1,0:T(8,128)(2,1)S(1)} %get-tuple-element.8.own_ref, bf16[2,1024,512]{2,1,0:T(8,128)(2,1)S(1)} %spread_weights.1.weights_ref, bf16[528,512]{1,0:T(8,128)(2,1)S(1)} %collective-permute-done.2.column_ref, f32[3,2,128]{2,1,0:T(2,128)S(1)} %pairs_inner.1.before_ref), custom_call_target="tpu_custom_call" | custom-call | flops 805306368 | bytes 2097152 | tf_op jit(solution)/shard_map/pairs_outer/pallas_call | solution.py:207
  (5 shorter events, 0.0 us)
Async XLA Ops:
  0.0 0.9 %copy-start = (bf16[1,2,128,256]{3,2,1,0:T(8,128)(2,1)S(1)}, bf16[1,2,128,256]{3,2,1,0:T(8,128)(2,1)}, u32[]{:S(2)}) copy-start(bf16[1,2,128,256]{3,2,1,0:T(8,128)(2,1)} %param.8) | copy-start | bytes 393220
  0.9 0.9 %copy-start.1 = (bf16[1,2,128,256]{3,2,1,0:T(8,128)(2,1)S(1)}, bf16[1,2,128,256]{3,2,1,0:T(8,128)(2,1)}, u32[]{:S(2)}) copy-start(bf16[1,2,128,256]{3,2,1,0:T(8,128)(2,1)} %param.9) | copy-start | bytes 393220
  1.8 0.9 %copy-start.2 = (bf16[256,256]{1,0:T(8,128)(2,1)S(1)}, bf16[256,256]{1,0:T(8,128)(2,1)}, u32[]{:S(2)}) copy-start(bf16[256,256]{1,0:T(8,128)(2,1)} %w_in_ref.1) | copy-start | bytes 393220
  2.7 0.9 %copy-start.3 = (bf16[256,256]{1,0:T(8,128)(2,1)S(1)}, bf16[256,256]{1,0:T(8,128)(2,1)}, u32[]{:S(2)}) copy-start(bf16[256,256]{1,0:T(8,128)(2,1)} %w_out_ref.1) | copy-start | bytes 393220
  3.6 0.7 %copy-start.5 = (bf16[1,2,3,128]{3,1,2,0:T(2,128)(2,1)S(1)}, bf16[1,2,3,128]{3,1,2,0:T(2,128)(2,1)}, u32[]{:S(2)}) copy-start(bf16[1,2,3,128]{3,1,2,0:T(2,128)(2,1)} %param.7) | copy-start | bytes 4612
  4.3 0.7 %copy-start.6 = (s32[1,2]{1,0:T(1,128)S(1)}, s32[1,2]{1,0:T(1,128)}, u32[]{:S(2)}) copy-start(s32[1,2]{1,0:T(1,128)} %counts_ref.1) | copy-start | bytes 28
  5.8 10.3 %collective-permute-start = (bf16[144,512]{1,0:T(8,128)(2,1)S(1)}, bf16[144,512]{1,0:T(8,128)(2,1)S(1)}, u32[]{:S(2)}, u32[]{:S(2)}) collective-permute-start(bf16[144,512]{1,0:T(8,128)(2,1)S(1)} %get-tuple-element.9), channel_id=1, source_target_pairs={{0,1},{1,0},{2,3},{3,2},{4,5},{5,4},{6,7},{7,6},{8,9},{9,8},{10,11... | collective-permute-start | bytes 442376 | tf_op jit(solution)/shard_map/ppermute | solution.py:165
  9.8 9.5 %collective-permute-start.1 = (bf16[144,512]{1,0:T(8,128)(2,1)S(1)}, bf16[144,512]{1,0:T(8,128)(2,1)S(1)}, u32[]{:S(2)}, u32[]{:S(2)}) collective-permute-start(bf16[144,512]{1,0:T(8,128)(2,1)S(1)} %get-tuple-element.10), channel_id=1, source_target_pairs={{0,7},{1,2},{2,1},{3,4},{4,3},{5,6},{6,5},{7,0},{8,15},{9,10},{10,... | collective-permute-start | bytes 442376 | tf_op jit(solution)/shard_map/ppermute | solution.py:165
  19.4 13.1 %collective-permute-start.3 = (bf16[528,512]{1,0:T(8,128)(2,1)S(1)}, bf16[528,512]{1,0:T(8,128)(2,1)}, u32[]{:S(2)}, u32[]{:S(2)}) collective-permute-start(bf16[528,512]{1,0:T(8,128)(2,1)S(1)} %join.1.column_ref), channel_id=1, source_target_pairs={{0,8},{8,0},{16,24},{24,16},{32,40},{40,32},{48,56},{56,48},{64,72... | collective-permute-start | bytes 1622024 | tf_op jit(solution)/shard_map/ppermute | solution.py:165
  27.2 16.5 %collective-permute-start.2 = (bf16[528,512]{1,0:T(8,128)(2,1)S(1)}, bf16[528,512]{1,0:T(8,128)(2,1)S(1)}, u32[]{:S(2)}, u32[]{:S(2)}) collective-permute-start(bf16[528,512]{1,0:T(8,128)(2,1)S(1)} %join.1.column_ref), channel_id=1, source_target_pairs={{0,504},{8,16},{16,8},{24,32},{32,24},{40,48},{48,40},{56,64},{64,... | collective-permute-start | bytes 1622024 | tf_op jit(solution)/shard_map/ppermute | solution.py:165
  29.2 0.7 %copy-start.4 = (bf16[8,256]{1,0:T(8,128)(2,1)S(1)}, bf16[8,256]{1,0:T(8,128)(2,1)}, u32[]{:S(2)}) copy-start(bf16[8,256]{1,0:T(8,128)(2,1)} %w_filter_ref.1) | copy-start | bytes 12292

commit v2 on v1

v2 whole, which is shorter than its diff:
```python
import math

import jax
import jax.numpy as jnp
from jax import lax
from jax.experimental import pallas as pl
from jax.experimental.pallas import tpu as pltpu
from jax.sharding import PartitionSpec as P

PITCH = 12.5
CUTOFF = 5.0
CENTER_STEP = 3.125
GAMMA = 0.2
FORCE_UNIT = 0.005
LOG2E = math.log2(math.e)

BOX = 128
F = 256
RADIAL = 8
MIDDLE = 4
ROWS = 16

LENGTH = PITCH / CUTOFF
SPREAD = GAMMA * CENTER_STEP**2
FACTORS = [math.exp(-SPREAD * (k - MIDDLE) ** 2) for k in range(RADIAL)]
OFFSET = 2.0 / CUTOFF**2 / (2.0 * GAMMA * CENTER_STEP)
SCALE = -2.0 * GAMMA * CENTER_STEP * CUTOFF * 2.0 * FORCE_UNIT

NN = (((1,), (0,)), ((), ()))
NT = (((1,), (1,)), ((), ()))
BF16 = jnp.bfloat16
F32 = jnp.float32


def vmem():
    return pl.BlockSpec(memory_space=pltpu.VMEM)


def hbm():
    return pl.BlockSpec(memory_space=pltpu.HBM)


def params(mib):
    return pltpu.CompilerParams(vmem_limit_bytes=mib * 2**20)


def shape(*dims, dtype=F32):
    return jax.ShapeDtypeStruct(dims, dtype)


def packed_offsets(rows):
    tall = jnp.concatenate([rows, jnp.zeros((16 - rows.shape[0], BOX), F32)], axis=0)
    wide = jnp.concatenate([tall, jnp.zeros((16, 2 * F - BOX), F32)], axis=1)
    return wide.astype(BF16)


def prepare(
    counts_ref, offsets_ref, features_ref, cotangent_ref, w_in_ref, w_out_ref, w_filter_ref,
    own_ref, first_ref, second_ref, filter_ref,
    counts, offsets_in, features, cotangent, w_in, w_out, sems,
):
    moves = [
        pltpu.make_async_copy(source, target, sems.at[i])
        for i, (source, target) in enumerate(
            [
                (features_ref, features), (w_in_ref, w_in), (cotangent_ref, cotangent), (w_out_ref, w_out),
                (counts_ref, counts), (offsets_ref, offsets_in), (w_filter_ref, filter_ref),
            ]
        )
    ]
    for move in moves:
        move.start()
    for move in moves:
        move.wait()
    odd = lax.rem(lax.axis_index("tower"), 2) == 1
    slots = lax.broadcasted_iota(jnp.int32, (BOX, F), 0)
    offsets = offsets_in[...].astype(F32)
    boxes = []
    for b in range(2):
        live = slots < counts[0, b]
        values = jnp.dot(features[b], w_in[...], preferred_element_type=F32)
        grads = lax.dot_general(cotangent[b], w_out[...], NT, preferred_element_type=F32)
        both = jnp.concatenate([jnp.where(live, values, 0.0), jnp.where(live, grads, 0.0)], axis=1)
        boxes.append(both)
        own_ref[b * BOX : (b + 1) * BOX, :] = both.astype(BF16)
    own_ref[2 * BOX :, :] = packed_offsets(offsets.reshape(6, BOX))
    first_ref[:BOX, :] = jnp.where(odd, boxes[0], boxes[1]).astype(BF16)
    second_ref[:BOX, :] = jnp.where(odd, boxes[1], boxes[0]).astype(BF16)
    first_ref[BOX:, :] = packed_offsets(jnp.where(odd, offsets[:, 0], offsets[:, 1]))
    second_ref[BOX:, :] = packed_offsets(jnp.where(odd, offsets[:, 1], offsets[:, 0]))


def join(second_ref, first_ref, outer_ref):
    odd = lax.rem(lax.axis_index("tower"), 2) == 1
    first = first_ref[...].astype(F32)
    second = second_ref[...].astype(F32)
    below = jnp.where(odd, first, second)
    above = jnp.where(odd, second, first)
    outer_ref[:BOX, :] = below[:BOX].astype(BF16)
    outer_ref[BOX : 2 * BOX, :] = above[:BOX].astype(BF16)
    rows = []
    for c in range(3):
        rows += [below[BOX + c : BOX + c + 1, :BOX], above[BOX + c : BOX + c + 1, :BOX]]
    outer_ref[2 * BOX :, :] = packed_offsets(jnp.concatenate(rows, axis=0))


def strengths(dx, dy, dz, a):
    c = jnp.maximum(1.0 - (dx * dx + dy * dy + dz * dz), 0.0)
    h = MIDDLE - RADIAL * c
    middle = jnp.exp2(h * h * (-SPREAD * LOG2E))
    up = jnp.exp2(h * (2.0 * SPREAD * LOG2E))
    down = jnp.exp2(h * (-2.0 * SPREAD * LOG2E))
    s = up * a[7]
    d = s
    p = a[6] + s
    for k in (5, 4):
        s = up * p
        d = up * d + s
        p = a[k] + s
    s = down * a[0]
    e = s
    for k in (1, 2, 3):
        s = down * (a[k] + s)
        e = down * e + s
    p = p + s
    d = d - e
    return (middle * c) * ((h * c + OFFSET) * p - c * d)


def rows_of(ref):
    return ref[2 * BOX :, :BOX].astype(F32) * LENGTH


def columns_of(ref):
    rows = rows_of(ref)
    return jnp.transpose(jnp.concatenate([rows, jnp.zeros((BOX - 16, BOX), F32)], axis=0))


def box_of(ref, b):
    return ref[b * BOX : (b + 1) * BOX, :]


def targets(rows, b, shifts):
    return [rows[2 * c + b : 2 * c + b + 1] - shifts[c] * LENGTH for c in range(3)]


def sources(columns, b, r):
    return [jnp.broadcast_to(columns[r : r + ROWS, 2 * c + b : 2 * c + b + 1], (ROWS, BOX)) for c in range(3)]


def zeros():
    return [jnp.zeros((ROWS, BOX), F32) for _ in range(3)]


def tile(product, r):
    return [product[r : r + ROWS, k * BOX : (k + 1) * BOX] for k in range(RADIAL)]


def total(t):
    return jnp.sum(t, axis=0, keepdims=True) * SCALE


def spread(own_ref, w_filter_ref, weights_ref):
    w = jnp.transpose(
        jnp.concatenate([w_filter_ref[...].astype(F32), jnp.zeros((BOX - RADIAL, F), F32)], axis=0)
    )
    for b in range(2):
        both = jnp.transpose(box_of(own_ref, b).astype(F32))
        for k in range(RADIAL):
            column = jnp.broadcast_to(w[:, k : k + 1] * FACTORS[k], (F, BOX))
            weights_ref[b, :F, k * BOX : (k + 1) * BOX] = (both[F:] * column).astype(BF16)
            weights_ref[b, F:, k * BOX : (k + 1) * BOX] = (both[:F] * column).astype(BF16)


def within(own_ref, w_filter_ref, weights_ref, forces_ref):
    spread(own_ref, w_filter_ref, weights_ref)
    rows, columns = rows_of(own_ref), columns_of(own_ref)
    sums = [zeros(), zeros()]
    for s in range(2):
        products = [
            lax.dot_general(box_of(own_ref, s), weights_ref[b], NN, preferred_element_type=F32) for b in range(2)
        ]
        mine = [targets(rows, b, (0.0, float(s - b), 0.0)) for b in range(2)]
        for r in range(0, BOX, ROWS):
            theirs = sources(columns, s, r)
            for b in range(2):
                along = [t - m for t, m in zip(theirs, mine[b], strict=True)]
                strength = strengths(*along, tile(products[b], r))
                sums[b] = [t + strength * a for t, a in zip(sums[b], along, strict=True)]
    for c in range(3):
        forces_ref[c] = jnp.concatenate([total(sums[0][c]), total(sums[1][c])], axis=0)


def across(own_ref, outer_ref, before_ref, w_filter_ref, weights_ref, so_far_ref, forces_ref, back_ref, filtered, turned):
    lane = lax.broadcasted_iota(jnp.int32, (ROWS, BOX), 1)
    own, outer, columns = rows_of(own_ref), rows_of(outer_ref), columns_of(before_ref)
    sums = [zeros(), zeros()]
    for s in range(2):
        source = box_of(before_ref, s)
        products = [lax.dot_general(source, weights_ref[b], NN, preferred_element_type=F32) for b in range(2)]
        wide = source.astype(F32)
        for k in range(RADIAL):
            w = w_filter_ref[k : k + 1, :].astype(F32) * FACTORS[k]
            filtered[s, k * BOX : (k + 1) * BOX, :F] = (wide[:, F:] * w).astype(BF16)
            filtered[s, k * BOX : (k + 1) * BOX, F:] = (wide[:, :F] * w).astype(BF16)
        corner = lax.dot_general(filtered[s], box_of(outer_ref, s), NT, preferred_element_type=F32)
        mine = [targets(own, b, (-1.0, float(s - b), 0.0)) for b in range(2)]
        diagonal = targets(outer, s, (-1.0, 1.0 - 2.0 * s, 0.0))
        for r in range(0, BOX, ROWS):
            theirs = sources(columns, s, r)
            along = [t - m for t, m in zip(theirs, diagonal, strict=True)]
            strength = strengths(*along, [corner[k * BOX + r : k * BOX + r + ROWS] for k in range(RADIAL)])
            back = [strength * a for a in along]
            for b in range(2):
                along = [t - m for t, m in zip(theirs, mine[b], strict=True)]
                strength = strengths(*along, tile(products[b], r))
                terms = [strength * a for a in along]
                sums[b] = [t + u for t, u in zip(sums[b], terms, strict=True)]
                back = [t + u for t, u in zip(back, terms, strict=True)]
            x, y, z = [jnp.sum(t, axis=1, keepdims=True) * -SCALE for t in back]
            turned[s, r : r + ROWS, :] = jnp.where(lane == 0, x, jnp.where(lane == 1, y, z))
    for c in range(3):
        forces_ref[c] = so_far_ref[c] + jnp.concatenate([total(sums[0][c]), total(sums[1][c])], axis=0)
    backs = [jnp.transpose(turned[s]) for s in range(2)]
    for c in range(3):
        back_ref[c] = jnp.concatenate([backs[s][c : c + 1] for s in range(2)], axis=0)


def outer_pairs(own_ref, outer_ref, weights_ref, shift):
    rows, columns = rows_of(own_ref), columns_of(outer_ref)
    sums = []
    for s in range(2):
        product = lax.dot_general(box_of(outer_ref, s), weights_ref[s], NN, preferred_element_type=F32)
        mine = targets(rows, s, (shift, 2.0 * s - 1.0, 0.0))
        t = zeros()
        for r in range(0, BOX, ROWS):
            along = [u - m for u, m in zip(sources(columns, s, r), mine, strict=True)]
            strength = strengths(*along, tile(product, r))
            t = [u + strength * a for u, a in zip(t, along, strict=True)]
        sums.append(t)
    return [jnp.concatenate([total(sums[0][c]), total(sums[1][c])], axis=0) for c in range(3)]


def beside(own_ref, outer_ref, weights_ref, so_far_ref, forces_ref):
    added = outer_pairs(own_ref, outer_ref, weights_ref, 0.0)
    for c in range(3):
        forces_ref[c] = so_far_ref[c] + added[c]


def finish(own_ref, outer_ref, weights_ref, so_far_ref, returned_ref, forces_ref):
    added = outer_pairs(own_ref, outer_ref, weights_ref, -1.0)
    for c in range(3):
        forces_ref[c] = (so_far_ref[c] + returned_ref[c]) + added[c]


def swap(x, axis, later):
    n = lax.axis_size(axis)
    if later:
        perm = [(i, (i + 1) % n if i % 2 else (i - 1) % n) for i in range(n)]
    else:
        perm = [(i, i + 1 - 2 * (i % 2)) for i in range(n)]
    return lax.ppermute(x, axis, perm)


def pass_on(x, axis, step):
    n = lax.axis_size(axis)
    return lax.ppermute(x, axis, [(i, (i + step) % n) for i in range(n)])


def kernel(body, name, out_shape, n_in, pair_count=0, scratch_shapes=()):
    return pl.pallas_call(
        body,
        out_shape=out_shape,
        in_specs=[vmem()] * n_in,
        out_specs=jax.tree.map(lambda _: vmem(), out_shape),
        scratch_shapes=list(scratch_shapes),
        compiler_params=params(40),
        cost_estimate=pl.CostEstimate(flops=pair_count * 2**27, bytes_accessed=2**18, transcendentals=0),
        name=name,
    )


def on_device(offsets, features, cotangent, w_in, w_out, w_filter, counts):
    turned = jnp.transpose(offsets[0], (1, 0, 2))
    forces_shape = shape(3, 2, BOX)
    own, first, second, filters = pl.pallas_call(
        prepare,
        out_shape=(
            shape(2 * BOX + 16, 2 * F, dtype=BF16),
            shape(BOX + 16, 2 * F, dtype=BF16),
            shape(BOX + 16, 2 * F, dtype=BF16),
            shape(RADIAL, F, dtype=BF16),
        ),
        in_specs=[hbm()] * 7,
        out_specs=(vmem(),) * 4,
        scratch_shapes=[
            pltpu.SMEM((1, 2), jnp.int32),
            pltpu.VMEM((3, 2, BOX), BF16),
            pltpu.VMEM((2, BOX, F), BF16),
            pltpu.VMEM((2, BOX, F), BF16),
            pltpu.VMEM((F, F), BF16),
            pltpu.VMEM((F, F), BF16),
            pltpu.SemaphoreType.DMA((7,)),
        ],
        compiler_params=params(16),
        name="prepare",
    )(*[pltpu.with_memory_space_constraint(x, pltpu.HBM) for x in (counts, turned, features[0], cotangent[0], w_in, w_out, w_filter)])
    second = swap(second, "tower", True)
    before = pass_on(own, "plane", 1)
    first = swap(first, "tower", False)
    weights, forces = kernel(
        within, "within", (shape(2, 2 * F, RADIAL * BOX, dtype=BF16), forces_shape), 2, 4
    )(own, filters)
    outer = kernel(join, "join", shape(2 * BOX + 16, 2 * F, dtype=BF16), 2)(second, first)
    before_outer = pass_on(outer, "plane", 1)
    forces, back = kernel(
        across,
        "across",
        (forces_shape, forces_shape),
        6,
        8,
        [pltpu.VMEM((2, RADIAL * BOX, 2 * F), BF16), pltpu.VMEM((2, BOX, BOX), F32)],
    )(own, outer, before, filters, weights, forces)
    returned = pass_on(back, "plane", -1)
    forces = kernel(beside, "beside", forces_shape, 4, 2)(own, outer, weights, forces)
    forces = kernel(finish, "finish", forces_shape, 5, 2)(own, before_outer, weights, forces, returned)
    return jnp.transpose(forces, (1, 0, 2))[None]


def solution(mesh):
    placed = (
        P("plane", "tower", None, None),
        P("plane", "tower", None, None),
        P("plane", "tower", None, None),
        P(),
        P(),
        P(),
        P("plane", "tower"),
    )
    return jax.shard_map(
        on_device,
        mesh=mesh,
        in_specs=placed,
        out_specs=P("plane", "tower", None, None),
        check_vma=False,
    )
```

time: 47 us -> 33.1 us (0.70)
  waiting for transfers between devices: 11 us -> 1.54 us
  local copies, waits for them, and re-layouts: 5.63 us -> 0 us
  starting transfers between devices: 20.1 us -> 24.6 us
  Pallas kernels: 9.89 us -> 6.47 us
    ppermute x0 -> x3, starting transfers between devices: none -> 14.7 us  [pass_on(): return lax.ppermute(x, axis, [(i, (i + step) % n) for i in range(n)])]
    ppermute x4 -> x2, starting transfers between devices: 20.1 us -> 9.85 us  [swap(): return lax.ppermute(x, axis, perm)]
    ppermute x4 -> x2, waiting for transfers between devices: 11 us -> 1.29 us  [swap(): return lax.ppermute(x, axis, perm)]
    unnamed x14 -> x0, local copies, waits for them, and re-layouts: 5.63 us -> none
    pallas_call x6, Pallas kernels: 9.89 us -> 6.47 us  [the longest x1 1.76 us: on_device(): kernel(across, 'across', (forces_shape, forces_shape), 6, 8, [pltpu.VMEM(...]
  transfers between devices with their start and end apart: 4 -> 5, of which waited for: 2 -> 2; matrix products, arithmetic and copies ran while one was open for 0% -> 0% of each run, Pallas kernels for 13% -> 12%
where the time goes in v2:
time: 33.1 us; the launch traced here: 32.7 us
  starting transfers between devices  24.6 us (74%)
  Pallas kernels  6.47 us (20%)
  waiting for transfers between devices  1.54 us (5%)
    ppermute x3, starting transfers between devices, pass_on(): return lax.ppermute(x, axis, [(i, (i + step) % n) for i in range(n)])  14.7 us
    ppermute x2, starting transfers between devices, swap(): return lax.ppermute(x, axis, perm)  9.85 us
    pallas_call x1, Pallas kernels, on_device(): kernel(across, 'across', (forces_shape, forces_shape), 6, 8, [pltpu.VMEM(...  1.76 us
    pallas_call x1, Pallas kernels, on_device(): kernel(within, 'within', (shape(2, 2 * F, RADIAL * BOX, dtype=BF16), forc...  1.52 us
    pallas_call x1, Pallas kernels, on_device(): pl.pallas_call(prepare, out_shape=(shape(2 * BOX + 16, 2 * F, dtype=BF16)...  1.44 us
    ppermute x2, waiting for transfers between devices, swap(): return lax.ppermute(x, axis, perm)  1.29 us
    pallas_call x1, Pallas kernels, on_device(): kernel(finish, 'finish', forces_shape, 5, 2)  1.12 us
  transfers between devices with their start and end apart: 5, of which 2 were waited for; matrix products, arithmetic and copies ran while one was open for 0% of the time, Pallas kernels for 12%

profile of v2, /device:TPU:1, one launch (start us, length us, event | category | flops | bytes accessed | tf_op | source)
XLA Modules:
  0.0 32.7 jit_solution(10125752125547429759)
XLA Ops:
  0.0 1.4 %prepare.1 = (bf16[272,512]{1,0:T(8,128)(2,1)S(1)}, bf16[144,512]{1,0:T(8,128)(2,1)S(1)}, bf16[144,512]{1,0:T(8,128)(2,1)S(1)}, bf16[8,256]{1,0:T(8,128)(2,1)S(1)}) custom-call(s32[1,2]{1,0:T(1,128)} %counts_ref.1, bf16[3,2,128]{2,1,0:T(2,128)(2,1)} %bitcast.10, bf16[2,128,256]{2,1,0:T(8,128)(2,1)} %bitcast.8, bf16[2,128,256]{2,1,0:T(8,128)(2,1)} %bitcast.9, ...), custom_call_target="tpu_custom_call" | custom-call | tf_op jit(solution)/shard_map/prepare/pallas_call | solution.py:286
  1.5 7.9 %collective-permute-start = (bf16[144,512]{1,0:T(8,128)(2,1)S(1)}, bf16[144,512]{1,0:T(8,128)(2,1)S(1)}, u32[]{:S(2)}, u32[]{:S(2)}) collective-permute-start(bf16[144,512]{1,0:T(8,128)(2,1)S(1)} %get-tuple-element.14), channel_id=1, source_target_pairs={{0,7},{1,2},{2,1},{3,4},{4,3},{5,6},{6,5},{7,0},{8,15},{9,10},{10,... | collective-permute-start | bytes 442376 | tf_op jit(solution)/shard_map/ppermute | solution.py:262
  9.4 1.9 %collective-permute-start.1 = (bf16[144,512]{1,0:T(8,128)(2,1)S(1)}, bf16[144,512]{1,0:T(8,128)(2,1)S(1)}, u32[]{:S(2)}, u32[]{:S(2)}) collective-permute-start(bf16[144,512]{1,0:T(8,128)(2,1)S(1)} %get-tuple-element.15), channel_id=1, source_target_pairs={{0,1},{1,0},{2,3},{3,2},{4,5},{5,4},{6,7},{7,6},{8,9},{9,8},{10,11... | collective-permute-start | bytes 442376 | tf_op jit(solution)/shard_map/ppermute | solution.py:262
  11.3 3.1 %collective-permute-start.3 = (bf16[272,512]{1,0:T(8,128)(2,1)S(1)}, bf16[272,512]{1,0:T(8,128)(2,1)S(1)}, u32[]{:S(2)}, u32[]{:S(2)}) collective-permute-start(bf16[272,512]{1,0:T(8,128)(2,1)S(1)} %get-tuple-element.13.own_ref), channel_id=1, source_target_pairs={{0,8},{8,16},{16,24},{24,32},{32,40},{40,48},{48,56},{56,64},{64,7... | collective-permute-start | bytes 835592 | tf_op jit(solution)/shard_map/ppermute | solution.py:267
  14.4 0.0 collective-permute-done.second_ref
  14.4 1.3 %collective-permute-done.1.first_ref = bf16[144,512]{1,0:T(8,128)(2,1)S(1)} collective-permute-done((bf16[144,512]{1,0:T(8,128)(2,1)S(1)}, bf16[144,512]{1,0:T(8,128)(2,1)S(1)}, u32[]{:S(2)}, u32[]{:S(2)}) %collective-permute-start.1) | collective-permute-done | bytes 147488 | tf_op jit(solution)/shard_map/ppermute | solution.py:262
  15.7 0.1 join.1.outer_ref
  15.8 4.0 %collective-permute-start.2 = (bf16[272,512]{1,0:T(8,128)(2,1)S(1)}, bf16[272,512]{1,0:T(8,128)(2,1)S(1)}, u32[]{:S(2)}, u32[]{:S(2)}) collective-permute-start(bf16[272,512]{1,0:T(8,128)(2,1)S(1)} %join.1.outer_ref), channel_id=1, source_target_pairs={{0,8},{8,16},{16,24},{24,32},{32,40},{40,48},{48,56},{56,64},{64,7... | collective-permute-start | bytes 835592 | tf_op jit(solution)/shard_map/ppermute | solution.py:267
  19.7 1.5 %within.1 = (bf16[2,512,1024]{2,1,0:T(8,128)(2,1)S(1)}, f32[3,2,128]{2,1,0:T(2,128)S(1)}) custom-call(bf16[272,512]{1,0:T(8,128)(2,1)S(1)} %get-tuple-element.13.own_ref, bf16[8,256]{1,0:T(8,128)(2,1)S(1)} %get-tuple-element.16.w_filter_ref), custom_call_target="tpu_custom_call" | custom-call | flops 536870912 | bytes 262144 | tf_op jit(solution)/shard_map/within/pallas_call | solution.py:311
  21.3 0.0 collective-permute-done.3.before_ref
  21.3 1.8 %across.1 = (f32[3,2,128]{2,1,0:T(2,128)S(1)}, f32[3,2,128]{2,1,0:T(2,128)S(1)}) custom-call(bf16[272,512]{1,0:T(8,128)(2,1)S(1)} %get-tuple-element.13.own_ref, bf16[272,512]{1,0:T(8,128)(2,1)S(1)} %join.1.outer_ref, bf16[272,512]{1,0:T(8,128)(2,1)S(1)} %collective-permute-done.3.before_ref, bf16[8,256]{1,0:T(8,128)(2,1)S(1)} %get-tuple-element.16.w_filter_ref, ...), custom_call_target="tpu_custom_call" | custom-call | flops 1073741824 | bytes 262144 | tf_op jit(solution)/shard_map/across/pallas_call | solution.py:316
  23.0 7.7 %collective-permute-start.4 = (f32[3,2,128]{2,1,0:T(2,128)S(1)}, f32[3,2,128]{2,1,0:T(2,128)S(1)}, u32[]{:S(2)}, u32[]{:S(2)}) collective-permute-start(f32[3,2,128]{2,1,0:T(2,128)S(1)} %get-tuple-element.20), channel_id=1, source_target_pairs={{0,504},{8,0},{16,8},{24,16},{32,24},{40,32},{48,40},{56,48},{64,5... | collective-permute-start | bytes 9224 | tf_op jit(solution)/shard_map/ppermute | solution.py:267
  30.8 0.5 %beside.1.so_far_ref = f32[3,2,128]{2,1,0:T(2,128)S(1)} custom-call(bf16[272,512]{1,0:T(8,128)(2,1)S(1)} %get-tuple-element.13.own_ref, bf16[272,512]{1,0:T(8,128)(2,1)S(1)} %join.1.outer_ref, bf16[2,512,1024]{2,1,0:T(8,128)(2,1)S(1)} %get-tuple-element.17.weights_ref, f32[3,2,128]{2,1,0:T(2,128)S(1)} %get-tuple-element.19.so_far_ref), custom_call_target="tpu_custom_call" | custom-call | flops 268435456 | bytes 262144 | tf_op jit(solution)/shard_map/beside/pallas_call | solution.py:325
  31.3 0.3 collective-permute-done.4.returned_ref
  31.6 0.0 collective-permute-done.2.outer_ref
  31.6 1.1 %finish.1 = f32[3,2,128]{2,1,0:T(2,128)} custom-call(bf16[272,512]{1,0:T(8,128)(2,1)S(1)} %get-tuple-element.13.own_ref, bf16[272,512]{1,0:T(8,128)(2,1)S(1)} %collective-permute-done.2.outer_ref, bf16[2,512,1024]{2,1,0:T(8,128)(2,1)S(1)} %get-tuple-element.17.weights_ref, f32[3,2,128]{2,1,0:T(2,128)S(1)} %beside.1.so_far_ref, ...), custom_call_target="tpu_custom_call" | custom-call | flops 268435456 | bytes 262144 | tf_op jit(solution)/shard_map/finish/pallas_call | solution.py:326
Async XLA Ops:
  1.5 12.9 %collective-permute-start = (bf16[144,512]{1,0:T(8,128)(2,1)S(1)}, bf16[144,512]{1,0:T(8,128)(2,1)S(1)}, u32[]{:S(2)}, u32[]{:S(2)}) collective-permute-start(bf16[144,512]{1,0:T(8,128)(2,1)S(1)} %get-tuple-element.14), channel_id=1, source_target_pairs={{0,7},{1,2},{2,1},{3,4},{4,3},{5,6},{6,5},{7,0},{8,15},{9,10},{10,... | collective-permute-start | bytes 442376 | tf_op jit(solution)/shard_map/ppermute | solution.py:262
  9.4 6.3 %collective-permute-start.1 = (bf16[144,512]{1,0:T(8,128)(2,1)S(1)}, bf16[144,512]{1,0:T(8,128)(2,1)S(1)}, u32[]{:S(2)}, u32[]{:S(2)}) collective-permute-start(bf16[144,512]{1,0:T(8,128)(2,1)S(1)} %get-tuple-element.15), channel_id=1, source_target_pairs={{0,1},{1,0},{2,3},{3,2},{4,5},{5,4},{6,7},{7,6},{8,9},{9,8},{10,11... | collective-permute-start | bytes 442376 | tf_op jit(solution)/shard_map/ppermute | solution.py:262
  11.3 10.0 %collective-permute-start.3 = (bf16[272,512]{1,0:T(8,128)(2,1)S(1)}, bf16[272,512]{1,0:T(8,128)(2,1)S(1)}, u32[]{:S(2)}, u32[]{:S(2)}) collective-permute-start(bf16[272,512]{1,0:T(8,128)(2,1)S(1)} %get-tuple-element.13.own_ref), channel_id=1, source_target_pairs={{0,8},{8,16},{16,24},{24,32},{32,40},{40,48},{48,56},{56,64},{64,7... | collective-permute-start | bytes 835592 | tf_op jit(solution)/shard_map/ppermute | solution.py:267
  15.8 15.8 %collective-permute-start.2 = (bf16[272,512]{1,0:T(8,128)(2,1)S(1)}, bf16[272,512]{1,0:T(8,128)(2,1)S(1)}, u32[]{:S(2)}, u32[]{:S(2)}) collective-permute-start(bf16[272,512]{1,0:T(8,128)(2,1)S(1)} %join.1.outer_ref), channel_id=1, source_target_pairs={{0,8},{8,16},{16,24},{24,32},{32,40},{40,48},{48,56},{56,64},{64,7... | collective-permute-start | bytes 835592 | tf_op jit(solution)/shard_map/ppermute | solution.py:267
  23.0 8.5 %collective-permute-start.4 = (f32[3,2,128]{2,1,0:T(2,128)S(1)}, f32[3,2,128]{2,1,0:T(2,128)S(1)}, u32[]{:S(2)}, u32[]{:S(2)}) collective-permute-start(f32[3,2,128]{2,1,0:T(2,128)S(1)} %get-tuple-element.20), channel_id=1, source_target_pairs={{0,504},{8,0},{16,8},{24,16},{32,24},{40,32},{48,40},{56,48},{64,5... | collective-permute-start | bytes 9224 | tf_op jit(solution)/shard_map/ppermute | solution.py:267

commit v3 on v2

--- a/solution.py
+++ b/solution.py
@@ -18,7 +18,8 @@
 F = 256
 RADIAL = 8
 MIDDLE = 4
-ROWS = 16
+ROWS = 32
+TAIL = 8
 
 LENGTH = PITCH / CUTOFF
 SPREAD = GAMMA * CENTER_STEP**2
@@ -49,8 +50,8 @@
 
 
 def packed_offsets(rows):
-    tall = jnp.concatenate([rows, jnp.zeros((16 - rows.shape[0], BOX), F32)], axis=0)
-    wide = jnp.concatenate([tall, jnp.zeros((16, 2 * F - BOX), F32)], axis=1)
+    tall = jnp.concatenate([rows, jnp.zeros((TAIL - rows.shape[0], BOX), F32)], axis=0)
+    wide = jnp.concatenate([tall, jnp.zeros((TAIL, 2 * F - BOX), F32)], axis=1)
     return wide.astype(BF16)
 
 
@@ -70,27 +71,27 @@
     ]
     for move in moves:
         move.start()
-    for move in moves:
-        move.wait()
-    odd = lax.rem(lax.axis_index("tower"), 2) == 1
+    odd = lax.rem(lax.axis_index("tower"), 2)
     slots = lax.broadcasted_iota(jnp.int32, (BOX, F), 0)
+    for i in (0, 1, 4):
+        moves[i].wait()
+    for b in range(2):
+        values = jnp.dot(features[b], w_in[...], preferred_element_type=F32)
+        own_ref[b * BOX : (b + 1) * BOX, :F] = jnp.where(slots < counts[0, b], values, 0.0).astype(BF16)
+    for i in (2, 3, 5, 6):
+        moves[i].wait()
+    for b in range(2):
+        grads = lax.dot_general(cotangent[b], w_out[...], NT, preferred_element_type=F32)
+        own_ref[b * BOX : (b + 1) * BOX, F:] = jnp.where(slots < counts[0, b], grads, 0.0).astype(BF16)
     offsets = offsets_in[...].astype(F32)
-    boxes = []
-    for b in range(2):
-        live = slots < counts[0, b]
-        values = jnp.dot(features[b], w_in[...], preferred_element_type=F32)
-        grads = lax.dot_general(cotangent[b], w_out[...], NT, preferred_element_type=F32)
-        both = jnp.concatenate([jnp.where(live, values, 0.0), jnp.where(live, grads, 0.0)], axis=1)
-        boxes.append(both)
-        own_ref[b * BOX : (b + 1) * BOX, :] = both.astype(BF16)
     own_ref[2 * BOX :, :] = packed_offsets(offsets.reshape(6, BOX))
-    first_ref[:BOX, :] = jnp.where(odd, boxes[0], boxes[1]).astype(BF16)
-    second_ref[:BOX, :] = jnp.where(odd, boxes[1], boxes[0]).astype(BF16)
-    first_ref[BOX:, :] = packed_offsets(jnp.where(odd, offsets[:, 0], offsets[:, 1]))
-    second_ref[BOX:, :] = packed_offsets(jnp.where(odd, offsets[:, 1], offsets[:, 0]))
-
-
-def join(second_ref, first_ref, outer_ref):
+    first_ref[:BOX, :] = own_ref[pl.ds(pl.multiple_of((1 - odd) * BOX, BOX), BOX), :]
+    second_ref[:BOX, :] = own_ref[pl.ds(pl.multiple_of(odd * BOX, BOX), BOX), :]
+    first_ref[BOX:, :] = packed_offsets(jnp.where(odd == 1, offsets[:, 0], offsets[:, 1]))
+    second_ref[BOX:, :] = packed_offsets(jnp.where(odd == 1, offsets[:, 1], offsets[:, 0]))
+
+
+def join(second_ref, first_ref, weights_ref, outer_ref):
     odd = lax.rem(lax.axis_index("tower"), 2) == 1
     first = first_ref[...].astype(F32)
     second = second_ref[...].astype(F32)
@@ -133,7 +134,7 @@
 
 def columns_of(ref):
     rows = rows_of(ref)
-    return jnp.transpose(jnp.concatenate([rows, jnp.zeros((BOX - 16, BOX), F32)], axis=0))
+    return jnp.transpose(jnp.concatenate([rows, jnp.zeros((BOX - TAIL, BOX), F32)], axis=0))
 
 
 def box_of(ref, b):
@@ -164,16 +165,15 @@
     w = jnp.transpose(
         jnp.concatenate([w_filter_ref[...].astype(F32), jnp.zeros((BOX - RADIAL, F), F32)], axis=0)
     )
-    for b in range(2):
-        both = jnp.transpose(box_of(own_ref, b).astype(F32))
-        for k in range(RADIAL):
-            column = jnp.broadcast_to(w[:, k : k + 1] * FACTORS[k], (F, BOX))
-            weights_ref[b, :F, k * BOX : (k + 1) * BOX] = (both[F:] * column).astype(BF16)
-            weights_ref[b, F:, k * BOX : (k + 1) * BOX] = (both[:F] * column).astype(BF16)
-
-
-def within(own_ref, w_filter_ref, weights_ref, forces_ref):
-    spread(own_ref, w_filter_ref, weights_ref)
+    turned = [jnp.transpose(box_of(own_ref, b).astype(F32)) for b in range(2)]
+    for k in range(RADIAL):
+        broad = jnp.broadcast_to(w[:, k : k + 1] * FACTORS[k], (F, BOX))
+        for b, both in enumerate(turned):
+            weights_ref[b, :F, k * BOX : (k + 1) * BOX] = (both[F:] * broad).astype(BF16)
+            weights_ref[b, F:, k * BOX : (k + 1) * BOX] = (both[:F] * broad).astype(BF16)
+
+
+def within(own_ref, weights_ref):
     rows, columns = rows_of(own_ref), columns_of(own_ref)
     sums = [zeros(), zeros()]
     for s in range(2):
@@ -187,22 +187,20 @@
                 along = [t - m for t, m in zip(theirs, mine[b], strict=True)]
                 strength = strengths(*along, tile(products[b], r))
                 sums[b] = [t + strength * a for t, a in zip(sums[b], along, strict=True)]
-    for c in range(3):
-        forces_ref[c] = jnp.concatenate([total(sums[0][c]), total(sums[1][c])], axis=0)
-
-
-def across(own_ref, outer_ref, before_ref, w_filter_ref, weights_ref, so_far_ref, forces_ref, back_ref, filtered, turned):
+    return [jnp.concatenate([total(sums[0][c]), total(sums[1][c])], axis=0) for c in range(3)]
+
+
+def across(own_ref, outer_ref, before_ref, w_filter_ref, so_far_ref, forces_ref, back_ref, filtered, turned):
     lane = lax.broadcasted_iota(jnp.int32, (ROWS, BOX), 1)
     own, outer, columns = rows_of(own_ref), rows_of(outer_ref), columns_of(before_ref)
     sums = [zeros(), zeros()]
     for s in range(2):
-        source = box_of(before_ref, s)
-        products = [lax.dot_general(source, weights_ref[b], NN, preferred_element_type=F32) for b in range(2)]
-        wide = source.astype(F32)
+        wide = box_of(before_ref, s).astype(F32)
         for k in range(RADIAL):
             w = w_filter_ref[k : k + 1, :].astype(F32) * FACTORS[k]
             filtered[s, k * BOX : (k + 1) * BOX, :F] = (wide[:, F:] * w).astype(BF16)
             filtered[s, k * BOX : (k + 1) * BOX, F:] = (wide[:, :F] * w).astype(BF16)
+        inner = lax.dot_general(filtered[s], own_ref[: 2 * BOX, :], NT, preferred_element_type=F32)
         corner = lax.dot_general(filtered[s], box_of(outer_ref, s), NT, preferred_element_type=F32)
         mine = [targets(own, b, (-1.0, float(s - b), 0.0)) for b in range(2)]
         diagonal = targets(outer, s, (-1.0, 1.0 - 2.0 * s, 0.0))
@@ -213,7 +211,10 @@
             back = [strength * a for a in along]
             for b in range(2):
                 along = [t - m for t, m in zip(theirs, mine[b], strict=True)]
-                strength = strengths(*along, tile(products[b], r))
+                strength = strengths(
+                    *along,
+                    [inner[k * BOX + r : k * BOX + r + ROWS, b * BOX : (b + 1) * BOX] for k in range(RADIAL)],
+                )
                 terms = [strength * a for a in along]
                 sums[b] = [t + u for t, u in zip(sums[b], terms, strict=True)]
                 back = [t + u for t, u in zip(back, terms, strict=True)]
@@ -241,16 +242,20 @@
     return [jnp.concatenate([total(sums[0][c]), total(sums[1][c])], axis=0) for c in range(3)]
 
 
-def beside(own_ref, outer_ref, weights_ref, so_far_ref, forces_ref):
-    added = outer_pairs(own_ref, outer_ref, weights_ref, 0.0)
+def column(own_ref, outer_ref, weights_ref, forces_ref):
+    near, far = within(own_ref, weights_ref), outer_pairs(own_ref, outer_ref, weights_ref, 0.0)
+    for c in range(3):
+        forces_ref[c] = near[c] + far[c]
+
+
+def corner(own_ref, outer_ref, weights_ref, so_far_ref, forces_ref):
+    added = outer_pairs(own_ref, outer_ref, weights_ref, -1.0)
     for c in range(3):
         forces_ref[c] = so_far_ref[c] + added[c]
 
 
-def finish(own_ref, outer_ref, weights_ref, so_far_ref, returned_ref, forces_ref):
-    added = outer_pairs(own_ref, outer_ref, weights_ref, -1.0)
-    for c in range(3):
-        forces_ref[c] = (so_far_ref[c] + returned_ref[c]) + added[c]
+def finish(so_far_ref, returned_ref, forces_ref):
+    forces_ref[...] = so_far_ref[...] + returned_ref[...]
 
 
 def swap(x, axis, later):
@@ -286,9 +291,9 @@
     own, first, second, filters = pl.pallas_call(
         prepare,
         out_shape=(
-            shape(2 * BOX + 16, 2 * F, dtype=BF16),
-            shape(BOX + 16, 2 * F, dtype=BF16),
-            shape(BOX + 16, 2 * F, dtype=BF16),
+            shape(2 * BOX + TAIL, 2 * F, dtype=BF16),
+            shape(BOX + TAIL, 2 * F, dtype=BF16),
+            shape(BOX + TAIL, 2 * F, dtype=BF16),
             shape(RADIAL, F, dtype=BF16),
         ),
         in_specs=[hbm()] * 7,
@@ -308,22 +313,21 @@
     second = swap(second, "tower", True)
     before = pass_on(own, "plane", 1)
     first = swap(first, "tower", False)
-    weights, forces = kernel(
-        within, "within", (shape(2, 2 * F, RADIAL * BOX, dtype=BF16), forces_shape), 2, 4
-    )(own, filters)
-    outer = kernel(join, "join", shape(2 * BOX + 16, 2 * F, dtype=BF16), 2)(second, first)
+    weights = kernel(spread, "spread", shape(2, 2 * F, RADIAL * BOX, dtype=BF16), 2, 0)(own, filters)
+    outer = kernel(join, "join", shape(2 * BOX + TAIL, 2 * F, dtype=BF16), 3)(second, first, weights)
     before_outer = pass_on(outer, "plane", 1)
+    forces = kernel(column, "column", forces_shape, 3, 2)(own, outer, weights)
     forces, back = kernel(
         across,
         "across",
         (forces_shape, forces_shape),
-        6,
+        5,
         8,
         [pltpu.VMEM((2, RADIAL * BOX, 2 * F), BF16), pltpu.VMEM((2, BOX, BOX), F32)],
-    )(own, outer, before, filters, weights, forces)
+    )(own, outer, before, filters, forces)
     returned = pass_on(back, "plane", -1)
-    forces = kernel(beside, "beside", forces_shape, 4, 2)(own, outer, weights, forces)
-    forces = kernel(finish, "finish", forces_shape, 5, 2)(own, before_outer, weights, forces, returned)
+    forces = kernel(corner, "corner", forces_shape, 4, 2)(own, before_outer, weights, forces)
+    forces = kernel(finish, "finish", forces_shape, 2)(forces, returned)
     return jnp.transpose(forces, (1, 0, 2))[None]
 
 

time: 33.1 us -> 32.2 us (0.973)
  waiting for transfers between devices: 1.54 us -> 0.6 us
  starting transfers between devices: 24.6 us -> 25 us
    ppermute x2, waiting for transfers between devices: 1.29 us -> 0.37 us  [swap(): return lax.ppermute(x, axis, perm)]
    ppermute x3, starting transfers between devices: 14.7 us -> 15.1 us  [pass_on(): return lax.ppermute(x, axis, [(i, (i + step) % n) for i in range(n)])]
    pallas_call x6 -> x7, Pallas kernels: 6.47 us -> 6.34 us  [the longest x1 1.66 us: on_device(): kernel(across, 'across', (forces_shape, forces_shape), 5, 8, [pltpu.VMEM(...]
  transfers between devices with their start and end apart: 5 -> 5, of which waited for: 2 -> 2; matrix products, arithmetic and copies ran while one was open for 0% -> 0% of each run, Pallas kernels for 12% -> 13%
where the time goes in v3:
time: 32.2 us; the launch traced here: 32 us
  starting transfers between devices  25 us (78%)
  Pallas kernels  6.34 us (20%)
  waiting for transfers between devices  0.6 us (2%)
    ppermute x3, starting transfers between devices, pass_on(): return lax.ppermute(x, axis, [(i, (i + step) % n) for i in range(n)])  15.1 us
    ppermute x2, starting transfers between devices, swap(): return lax.ppermute(x, axis, perm)  9.85 us
    pallas_call x1, Pallas kernels, on_device(): kernel(across, 'across', (forces_shape, forces_shape), 5, 8, [pltpu.VMEM(...  1.66 us
    pallas_call x1, Pallas kernels, on_device(): pl.pallas_call(prepare, out_shape=(shape(2 * BOX + TAIL, 2 * F, dtype=BF1...  1.49 us
    pallas_call x1, Pallas kernels, on_device(): forces = kernel(column, 'column', forces_shape, 3, 2)(own, outer, weights)  1.24 us
    pallas_call x1, Pallas kernels, on_device(): kernel(spread, 'spread', shape(2, 2 * F, RADIAL * BOX, dtype=BF16), 2, 0)  0.73 us
  transfers between devices with their start and end apart: 5, of which 2 were waited for; matrix products, arithmetic and copies ran while one was open for 0% of the time, Pallas kernels for 13%

profile of v3, /device:TPU:1, one launch (start us, length us, event | category | flops | bytes accessed | tf_op | source)
XLA Modules:
  0.0 32.0 jit_solution(14634217064953704402)
XLA Ops:
  0.0 1.5 %prepare.1 = (bf16[264,512]{1,0:T(8,128)(2,1)S(1)}, bf16[136,512]{1,0:T(8,128)(2,1)S(1)}, bf16[136,512]{1,0:T(8,128)(2,1)S(1)}, bf16[8,256]{1,0:T(8,128)(2,1)S(1)}) custom-call(s32[1,2]{1,0:T(1,128)} %counts_ref.1, bf16[3,2,128]{2,1,0:T(2,128)(2,1)} %bitcast.10, bf16[2,128,256]{2,1,0:T(8,128)(2,1)} %bitcast.8, bf16[2,128,256]{2,1,0:T(8,128)(2,1)} %bitcast.9, ...), custom_call_target="tpu_custom_call" | custom-call | tf_op jit(solution)/shard_map/prepare/pallas_call | solution.py:291
  1.5 7.9 %collective-permute-start = (bf16[136,512]{1,0:T(8,128)(2,1)S(1)}, bf16[136,512]{1,0:T(8,128)(2,1)S(1)}, u32[]{:S(2)}, u32[]{:S(2)}) collective-permute-start(bf16[136,512]{1,0:T(8,128)(2,1)S(1)} %get-tuple-element.12), channel_id=1, source_target_pairs={{0,7},{1,2},{2,1},{3,4},{4,3},{5,6},{6,5},{7,0},{8,15},{9,10},{10,... | collective-permute-start | bytes 417800 | tf_op jit(solution)/shard_map/ppermute | solution.py:267
  9.4 1.9 %collective-permute-start.1 = (bf16[136,512]{1,0:T(8,128)(2,1)S(1)}, bf16[136,512]{1,0:T(8,128)(2,1)S(1)}, u32[]{:S(2)}, u32[]{:S(2)}) collective-permute-start(bf16[136,512]{1,0:T(8,128)(2,1)S(1)} %get-tuple-element.13), channel_id=1, source_target_pairs={{0,1},{1,0},{2,3},{3,2},{4,5},{5,4},{6,7},{7,6},{8,9},{9,8},{10,11... | collective-permute-start | bytes 417800 | tf_op jit(solution)/shard_map/ppermute | solution.py:267
  11.4 3.1 %collective-permute-start.3 = (bf16[264,512]{1,0:T(8,128)(2,1)S(1)}, bf16[264,512]{1,0:T(8,128)(2,1)S(1)}, u32[]{:S(2)}, u32[]{:S(2)}) collective-permute-start(bf16[264,512]{1,0:T(8,128)(2,1)S(1)} %get-tuple-element.11.own_ref), channel_id=1, source_target_pairs={{0,8},{8,16},{16,24},{24,32},{32,40},{40,48},{48,56},{56,64},{64,7... | collective-permute-start | bytes 811016 | tf_op jit(solution)/shard_map/ppermute | solution.py:272
  14.4 0.7 %spread.1.weights_ref = bf16[2,512,1024]{2,1,0:T(8,128)(2,1)S(1)} custom-call(bf16[264,512]{1,0:T(8,128)(2,1)S(1)} %get-tuple-element.11.own_ref, bf16[8,256]{1,0:T(8,128)(2,1)S(1)} %get-tuple-element.14.w_filter_ref), custom_call_target="tpu_custom_call" | custom-call | bytes 262144 | tf_op jit(solution)/shard_map/spread/pallas_call | solution.py:316
  15.2 0.0 collective-permute-done.second_ref
  15.2 0.4 %collective-permute-done.1.first_ref = bf16[136,512]{1,0:T(8,128)(2,1)S(1)} collective-permute-done((bf16[136,512]{1,0:T(8,128)(2,1)S(1)}, bf16[136,512]{1,0:T(8,128)(2,1)S(1)}, u32[]{:S(2)}, u32[]{:S(2)}) %collective-permute-start.1) | collective-permute-done | bytes 139296 | tf_op jit(solution)/shard_map/ppermute | solution.py:267
  15.6 0.1 join.1.outer_ref
  15.6 4.0 %collective-permute-start.2 = (bf16[264,512]{1,0:T(8,128)(2,1)S(1)}, bf16[264,512]{1,0:T(8,128)(2,1)S(1)}, u32[]{:S(2)}, u32[]{:S(2)}) collective-permute-start(bf16[264,512]{1,0:T(8,128)(2,1)S(1)} %join.1.outer_ref), channel_id=1, source_target_pairs={{0,8},{8,16},{16,24},{24,32},{32,40},{40,48},{48,56},{56,64},{64,7... | collective-permute-start | bytes 811016 | tf_op jit(solution)/shard_map/ppermute | solution.py:272
  19.6 1.2 %column.1.so_far_ref = f32[3,2,128]{2,1,0:T(2,128)S(1)} custom-call(bf16[264,512]{1,0:T(8,128)(2,1)S(1)} %get-tuple-element.11.own_ref, bf16[264,512]{1,0:T(8,128)(2,1)S(1)} %join.1.outer_ref, bf16[2,512,1024]{2,1,0:T(8,128)(2,1)S(1)} %spread.1.weights_ref), custom_call_target="tpu_custom_call" | custom-call | flops 268435456 | bytes 262144 | tf_op jit(solution)/shard_map/column/pallas_call | solution.py:319
  20.9 0.0 collective-permute-done.3.before_ref
  20.9 1.7 %across.1 = (f32[3,2,128]{2,1,0:T(2,128)S(1)}, f32[3,2,128]{2,1,0:T(2,128)S(1)}) custom-call(bf16[264,512]{1,0:T(8,128)(2,1)S(1)} %get-tuple-element.11.own_ref, bf16[264,512]{1,0:T(8,128)(2,1)S(1)} %join.1.outer_ref, bf16[264,512]{1,0:T(8,128)(2,1)S(1)} %collective-permute-done.3.before_ref, bf16[8,256]{1,0:T(8,128)(2,1)S(1)} %get-tuple-element.14.w_filter_ref, ...), custom_call_target="tpu_custom_call" | custom-call | flops 1073741824 | bytes 262144 | tf_op jit(solution)/shard_map/across/pallas_call | solution.py:320
  22.5 8.1 %collective-permute-start.4 = (f32[3,2,128]{2,1,0:T(2,128)S(1)}, f32[3,2,128]{2,1,0:T(2,128)S(1)}, u32[]{:S(2)}, u32[]{:S(2)}) collective-permute-start(f32[3,2,128]{2,1,0:T(2,128)S(1)} %get-tuple-element.16), channel_id=1, source_target_pairs={{0,504},{8,0},{16,8},{24,16},{32,24},{40,32},{48,40},{56,48},{64,5... | collective-permute-start | bytes 9224 | tf_op jit(solution)/shard_map/ppermute | solution.py:272
  30.6 0.0 collective-permute-done.2.outer_ref
  30.6 0.6 %corner.1.so_far_ref = f32[3,2,128]{2,1,0:T(2,128)S(1)} custom-call(bf16[264,512]{1,0:T(8,128)(2,1)S(1)} %get-tuple-element.11.own_ref, bf16[264,512]{1,0:T(8,128)(2,1)S(1)} %collective-permute-done.2.outer_ref, bf16[2,512,1024]{2,1,0:T(8,128)(2,1)S(1)} %spread.1.weights_ref, f32[3,2,128]{2,1,0:T(2,128)S(1)} %get-tuple-element.15.so_far_ref), custom_call_target="tpu_custom_call" | custom-call | flops 268435456 | bytes 262144 | tf_op jit(solution)/shard_map/corner/pallas_call | solution.py:329
  31.2 0.2 collective-permute-done.4.returned_ref
  31.4 0.6 %finish.1 = f32[3,2,128]{2,1,0:T(2,128)} custom-call(f32[3,2,128]{2,1,0:T(2,128)S(1)} %corner.1.so_far_ref, f32[3,2,128]{2,1,0:T(2,128)S(1)} %collective-permute-done.4.returned_ref), custom_call_target="tpu_custom_call" | custom-call | bytes 262144 | tf_op jit(solution)/shard_map/finish/pallas_call | solution.py:330
Async XLA Ops:
  1.5 13.7 %collective-permute-start = (bf16[136,512]{1,0:T(8,128)(2,1)S(1)}, bf16[136,512]{1,0:T(8,128)(2,1)S(1)}, u32[]{:S(2)}, u32[]{:S(2)}) collective-permute-start(bf16[136,512]{1,0:T(8,128)(2,1)S(1)} %get-tuple-element.12), channel_id=1, source_target_pairs={{0,7},{1,2},{2,1},{3,4},{4,3},{5,6},{6,5},{7,0},{8,15},{9,10},{10,... | collective-permute-start | bytes 417800 | tf_op jit(solution)/shard_map/ppermute | solution.py:267
  9.4 6.1 %collective-permute-start.1 = (bf16[136,512]{1,0:T(8,128)(2,1)S(1)}, bf16[136,512]{1,0:T(8,128)(2,1)S(1)}, u32[]{:S(2)}, u32[]{:S(2)}) collective-permute-start(bf16[136,512]{1,0:T(8,128)(2,1)S(1)} %get-tuple-element.13), channel_id=1, source_target_pairs={{0,1},{1,0},{2,3},{3,2},{4,5},{5,4},{6,7},{7,6},{8,9},{9,8},{10,11... | collective-permute-start | bytes 417800 | tf_op jit(solution)/shard_map/ppermute | solution.py:267
  11.4 9.5 %collective-permute-start.3 = (bf16[264,512]{1,0:T(8,128)(2,1)S(1)}, bf16[264,512]{1,0:T(8,128)(2,1)S(1)}, u32[]{:S(2)}, u32[]{:S(2)}) collective-permute-start(bf16[264,512]{1,0:T(8,128)(2,1)S(1)} %get-tuple-element.11.own_ref), channel_id=1, source_target_pairs={{0,8},{8,16},{16,24},{24,32},{32,40},{40,48},{48,56},{56,64},{64,7... | collective-permute-start | bytes 811016 | tf_op jit(solution)/shard_map/ppermute | solution.py:272
  15.6 15.0 %collective-permute-start.2 = (bf16[264,512]{1,0:T(8,128)(2,1)S(1)}, bf16[264,512]{1,0:T(8,128)(2,1)S(1)}, u32[]{:S(2)}, u32[]{:S(2)}) collective-permute-start(bf16[264,512]{1,0:T(8,128)(2,1)S(1)} %join.1.outer_ref), channel_id=1, source_target_pairs={{0,8},{8,16},{16,24},{24,32},{32,40},{40,48},{48,56},{56,64},{64,7... | collective-permute-start | bytes 811016 | tf_op jit(solution)/shard_map/ppermute | solution.py:272
  22.5 8.9 %collective-permute-start.4 = (f32[3,2,128]{2,1,0:T(2,128)S(1)}, f32[3,2,128]{2,1,0:T(2,128)S(1)}, u32[]{:S(2)}, u32[]{:S(2)}) collective-permute-start(f32[3,2,128]{2,1,0:T(2,128)S(1)} %get-tuple-element.16), channel_id=1, source_target_pairs={{0,504},{8,0},{16,8},{24,16},{32,24},{40,32},{48,40},{56,48},{64,5... | collective-permute-start | bytes 9224 | tf_op jit(solution)/shard_map/ppermute | solution.py:272

commit v4 on v3

--- a/solution.py
+++ b/solution.py
@@ -162,12 +162,12 @@
 
 
 def spread(own_ref, w_filter_ref, weights_ref):
-    w = jnp.transpose(
-        jnp.concatenate([w_filter_ref[...].astype(F32), jnp.zeros((BOX - RADIAL, F), F32)], axis=0)
-    )
+    lanes = lax.broadcasted_iota(jnp.int32, (RADIAL, RADIAL * BOX), 1) // BOX
+    picks = (lanes == lax.broadcasted_iota(jnp.int32, (RADIAL, RADIAL * BOX), 0)).astype(F32).astype(BF16)
+    w = lax.dot_general(w_filter_ref[...], picks, (((0,), (0,)), ((), ())), preferred_element_type=F32)
     turned = [jnp.transpose(box_of(own_ref, b).astype(F32)) for b in range(2)]
     for k in range(RADIAL):
-        broad = jnp.broadcast_to(w[:, k : k + 1] * FACTORS[k], (F, BOX))
+        broad = w[:, k * BOX : (k + 1) * BOX] * FACTORS[k]
         for b, both in enumerate(turned):
             weights_ref[b, :F, k * BOX : (k + 1) * BOX] = (both[F:] * broad).astype(BF16)
             weights_ref[b, F:, k * BOX : (k + 1) * BOX] = (both[:F] * broad).astype(BF16)
@@ -194,6 +194,7 @@
     lane = lax.broadcasted_iota(jnp.int32, (ROWS, BOX), 1)
     own, outer, columns = rows_of(own_ref), rows_of(outer_ref), columns_of(before_ref)
     sums = [zeros(), zeros()]
+    ready = []
     for s in range(2):
         wide = box_of(before_ref, s).astype(F32)
         for k in range(RADIAL):
@@ -202,6 +203,9 @@
             filtered[s, k * BOX : (k + 1) * BOX, F:] = (wide[:, :F] * w).astype(BF16)
         inner = lax.dot_general(filtered[s], own_ref[: 2 * BOX, :], NT, preferred_element_type=F32)
         corner = lax.dot_general(filtered[s], box_of(outer_ref, s), NT, preferred_element_type=F32)
+        ready.append((inner, corner))
+    for s in range(2):
+        inner, corner = ready[s]
         mine = [targets(own, b, (-1.0, float(s - b), 0.0)) for b in range(2)]
         diagonal = targets(outer, s, (-1.0, 1.0 - 2.0 * s, 0.0))
         for r in range(0, BOX, ROWS):

time: 32.2 us -> 32.2 us (level)
  no operation moved by 1% of the time
where the time goes in v4:
time: 32.2 us; the launch traced here: 32 us
  starting transfers between devices  25 us (78%)
  Pallas kernels  6.17 us (19%)
  waiting for transfers between devices  0.76 us (2%)
    ppermute x3, starting transfers between devices, pass_on(): return lax.ppermute(x, axis, [(i, (i + step) % n) for i in range(n)])  15.1 us
    ppermute x2, starting transfers between devices, swap(): return lax.ppermute(x, axis, perm)  9.85 us
    pallas_call x1, Pallas kernels, on_device(): kernel(across, 'across', (forces_shape, forces_shape), 5, 8, [pltpu.VMEM(...  1.66 us
    pallas_call x1, Pallas kernels, on_device(): pl.pallas_call(prepare, out_shape=(shape(2 * BOX + TAIL, 2 * F, dtype=BF1...  1.49 us
    pallas_call x1, Pallas kernels, on_device(): forces = kernel(column, 'column', forces_shape, 3, 2)(own, outer, weights)  1.24 us
  transfers between devices with their start and end apart: 5, of which 2 were waited for; matrix products, arithmetic and copies ran while one was open for 0% of the time, Pallas kernels for 13%

profile of v4, /device:TPU:1, one launch (start us, length us, event | category | flops | bytes accessed | tf_op | source)
XLA Modules:
  0.0 32.0 jit_solution(5860789792902854124)
XLA Ops:
  0.0 1.5 %prepare.1 = (bf16[264,512]{1,0:T(8,128)(2,1)S(1)}, bf16[136,512]{1,0:T(8,128)(2,1)S(1)}, bf16[136,512]{1,0:T(8,128)(2,1)S(1)}, bf16[8,256]{1,0:T(8,128)(2,1)S(1)}) custom-call(s32[1,2]{1,0:T(1,128)} %counts_ref.1, bf16[3,2,128]{2,1,0:T(2,128)(2,1)} %bitcast.10, bf16[2,128,256]{2,1,0:T(8,128)(2,1)} %bitcast.8, bf16[2,128,256]{2,1,0:T(8,128)(2,1)} %bitcast.9, ...), custom_call_target="tpu_custom_call" | custom-call | tf_op jit(solution)/shard_map/prepare/pallas_call | solution.py:295
  1.5 7.9 %collective-permute-start = (bf16[136,512]{1,0:T(8,128)(2,1)S(1)}, bf16[136,512]{1,0:T(8,128)(2,1)S(1)}, u32[]{:S(2)}, u32[]{:S(2)}) collective-permute-start(bf16[136,512]{1,0:T(8,128)(2,1)S(1)} %get-tuple-element.12), channel_id=1, source_target_pairs={{0,7},{1,2},{2,1},{3,4},{4,3},{5,6},{6,5},{7,0},{8,15},{9,10},{10,... | collective-permute-start | bytes 417800 | tf_op jit(solution)/shard_map/ppermute | solution.py:271
  9.4 1.9 %collective-permute-start.1 = (bf16[136,512]{1,0:T(8,128)(2,1)S(1)}, bf16[136,512]{1,0:T(8,128)(2,1)S(1)}, u32[]{:S(2)}, u32[]{:S(2)}) collective-permute-start(bf16[136,512]{1,0:T(8,128)(2,1)S(1)} %get-tuple-element.13), channel_id=1, source_target_pairs={{0,1},{1,0},{2,3},{3,2},{4,5},{5,4},{6,7},{7,6},{8,9},{9,8},{10,11... | collective-permute-start | bytes 417800 | tf_op jit(solution)/shard_map/ppermute | solution.py:271
  11.4 3.1 %collective-permute-start.3 = (bf16[264,512]{1,0:T(8,128)(2,1)S(1)}, bf16[264,512]{1,0:T(8,128)(2,1)S(1)}, u32[]{:S(2)}, u32[]{:S(2)}) collective-permute-start(bf16[264,512]{1,0:T(8,128)(2,1)S(1)} %get-tuple-element.11.own_ref), channel_id=1, source_target_pairs={{0,8},{8,16},{16,24},{24,32},{32,40},{40,48},{48,56},{56,64},{64,7... | collective-permute-start | bytes 811016 | tf_op jit(solution)/shard_map/ppermute | solution.py:276
  14.4 0.6 %spread.1.weights_ref = bf16[2,512,1024]{2,1,0:T(8,128)(2,1)S(1)} custom-call(bf16[264,512]{1,0:T(8,128)(2,1)S(1)} %get-tuple-element.11.own_ref, bf16[8,256]{1,0:T(8,128)(2,1)S(1)} %get-tuple-element.14.w_filter_ref), custom_call_target="tpu_custom_call" | custom-call | bytes 262144 | tf_op jit(solution)/shard_map/spread/pallas_call | solution.py:320
  15.0 0.0 collective-permute-done.second_ref
  15.0 0.5 %collective-permute-done.1.first_ref = bf16[136,512]{1,0:T(8,128)(2,1)S(1)} collective-permute-done((bf16[136,512]{1,0:T(8,128)(2,1)S(1)}, bf16[136,512]{1,0:T(8,128)(2,1)S(1)}, u32[]{:S(2)}, u32[]{:S(2)}) %collective-permute-start.1) | collective-permute-done | bytes 139296 | tf_op jit(solution)/shard_map/ppermute | solution.py:271
  15.6 0.1 join.1.outer_ref
  15.6 4.0 %collective-permute-start.2 = (bf16[264,512]{1,0:T(8,128)(2,1)S(1)}, bf16[264,512]{1,0:T(8,128)(2,1)S(1)}, u32[]{:S(2)}, u32[]{:S(2)}) collective-permute-start(bf16[264,512]{1,0:T(8,128)(2,1)S(1)} %join.1.outer_ref), channel_id=1, source_target_pairs={{0,8},{8,16},{16,24},{24,32},{32,40},{40,48},{48,56},{56,64},{64,7... | collective-permute-start | bytes 811016 | tf_op jit(solution)/shard_map/ppermute | solution.py:276
  19.6 1.2 %column.1.so_far_ref = f32[3,2,128]{2,1,0:T(2,128)S(1)} custom-call(bf16[264,512]{1,0:T(8,128)(2,1)S(1)} %get-tuple-element.11.own_ref, bf16[264,512]{1,0:T(8,128)(2,1)S(1)} %join.1.outer_ref, bf16[2,512,1024]{2,1,0:T(8,128)(2,1)S(1)} %spread.1.weights_ref), custom_call_target="tpu_custom_call" | custom-call | flops 268435456 | bytes 262144 | tf_op jit(solution)/shard_map/column/pallas_call | solution.py:323
  20.9 0.0 collective-permute-done.3.before_ref
  20.9 1.7 %across.1 = (f32[3,2,128]{2,1,0:T(2,128)S(1)}, f32[3,2,128]{2,1,0:T(2,128)S(1)}) custom-call(bf16[264,512]{1,0:T(8,128)(2,1)S(1)} %get-tuple-element.11.own_ref, bf16[264,512]{1,0:T(8,128)(2,1)S(1)} %join.1.outer_ref, bf16[264,512]{1,0:T(8,128)(2,1)S(1)} %collective-permute-done.3.before_ref, bf16[8,256]{1,0:T(8,128)(2,1)S(1)} %get-tuple-element.14.w_filter_ref, ...), custom_call_target="tpu_custom_call" | custom-call | flops 1073741824 | bytes 262144 | tf_op jit(solution)/shard_map/across/pallas_call | solution.py:324
  22.5 8.1 %collective-permute-start.4 = (f32[3,2,128]{2,1,0:T(2,128)S(1)}, f32[3,2,128]{2,1,0:T(2,128)S(1)}, u32[]{:S(2)}, u32[]{:S(2)}) collective-permute-start(f32[3,2,128]{2,1,0:T(2,128)S(1)} %get-tuple-element.16), channel_id=1, source_target_pairs={{0,504},{8,0},{16,8},{24,16},{32,24},{40,32},{48,40},{56,48},{64,5... | collective-permute-start | bytes 9224 | tf_op jit(solution)/shard_map/ppermute | solution.py:276
  30.6 0.0 collective-permute-done.2.outer_ref
  30.6 0.6 %corner.1.so_far_ref = f32[3,2,128]{2,1,0:T(2,128)S(1)} custom-call(bf16[264,512]{1,0:T(8,128)(2,1)S(1)} %get-tuple-element.11.own_ref, bf16[264,512]{1,0:T(8,128)(2,1)S(1)} %collective-permute-done.2.outer_ref, bf16[2,512,1024]{2,1,0:T(8,128)(2,1)S(1)} %spread.1.weights_ref, f32[3,2,128]{2,1,0:T(2,128)S(1)} %get-tuple-element.15.so_far_ref), custom_call_target="tpu_custom_call" | custom-call | flops 268435456 | bytes 262144 | tf_op jit(solution)/shard_map/corner/pallas_call | solution.py:333
  31.2 0.2 collective-permute-done.4.returned_ref
  31.4 0.6 %finish.1 = f32[3,2,128]{2,1,0:T(2,128)} custom-call(f32[3,2,128]{2,1,0:T(2,128)S(1)} %corner.1.so_far_ref, f32[3,2,128]{2,1,0:T(2,128)S(1)} %collective-permute-done.4.returned_ref), custom_call_target="tpu_custom_call" | custom-call | bytes 262144 | tf_op jit(solution)/shard_map/finish/pallas_call | solution.py:334
Async XLA Ops:
  1.5 13.5 %collective-permute-start = (bf16[136,512]{1,0:T(8,128)(2,1)S(1)}, bf16[136,512]{1,0:T(8,128)(2,1)S(1)}, u32[]{:S(2)}, u32[]{:S(2)}) collective-permute-start(bf16[136,512]{1,0:T(8,128)(2,1)S(1)} %get-tuple-element.12), channel_id=1, source_target_pairs={{0,7},{1,2},{2,1},{3,4},{4,3},{5,6},{6,5},{7,0},{8,15},{9,10},{10,... | collective-permute-start | bytes 417800 | tf_op jit(solution)/shard_map/ppermute | solution.py:271
  9.4 6.1 %collective-permute-start.1 = (bf16[136,512]{1,0:T(8,128)(2,1)S(1)}, bf16[136,512]{1,0:T(8,128)(2,1)S(1)}, u32[]{:S(2)}, u32[]{:S(2)}) collective-permute-start(bf16[136,512]{1,0:T(8,128)(2,1)S(1)} %get-tuple-element.13), channel_id=1, source_target_pairs={{0,1},{1,0},{2,3},{3,2},{4,5},{5,4},{6,7},{7,6},{8,9},{9,8},{10,11... | collective-permute-start | bytes 417800 | tf_op jit(solution)/shard_map/ppermute | solution.py:271
  11.4 9.5 %collective-permute-start.3 = (bf16[264,512]{1,0:T(8,128)(2,1)S(1)}, bf16[264,512]{1,0:T(8,128)(2,1)S(1)}, u32[]{:S(2)}, u32[]{:S(2)}) collective-permute-start(bf16[264,512]{1,0:T(8,128)(2,1)S(1)} %get-tuple-element.11.own_ref), channel_id=1, source_target_pairs={{0,8},{8,16},{16,24},{24,32},{32,40},{40,48},{48,56},{56,64},{64,7... | collective-permute-start | bytes 811016 | tf_op jit(solution)/shard_map/ppermute | solution.py:276
  15.6 15.0 %collective-permute-start.2 = (bf16[264,512]{1,0:T(8,128)(2,1)S(1)}, bf16[264,512]{1,0:T(8,128)(2,1)S(1)}, u32[]{:S(2)}, u32[]{:S(2)}) collective-permute-start(bf16[264,512]{1,0:T(8,128)(2,1)S(1)} %join.1.outer_ref), channel_id=1, source_target_pairs={{0,8},{8,16},{16,24},{24,32},{32,40},{40,48},{48,56},{56,64},{64,7... | collective-permute-start | bytes 811016 | tf_op jit(solution)/shard_map/ppermute | solution.py:276
  22.5 8.9 %collective-permute-start.4 = (f32[3,2,128]{2,1,0:T(2,128)S(1)}, f32[3,2,128]{2,1,0:T(2,128)S(1)}, u32[]{:S(2)}, u32[]{:S(2)}) collective-permute-start(f32[3,2,128]{2,1,0:T(2,128)S(1)} %get-tuple-element.16), channel_id=1, source_target_pairs={{0,504},{8,0},{16,8},{24,16},{32,24},{40,32},{48,40},{56,48},{64,5... | collective-permute-start | bytes 9224 | tf_op jit(solution)/shard_map/ppermute | solution.py:276

commit v5 on v4

--- a/solution.py
+++ b/solution.py
@@ -173,21 +173,26 @@
             weights_ref[b, F:, k * BOX : (k + 1) * BOX] = (both[:F] * broad).astype(BF16)
 
 
-def within(own_ref, weights_ref):
-    rows, columns = rows_of(own_ref), columns_of(own_ref)
+def within(own_ref, weights_ref, turned):
+    lane = lax.broadcasted_iota(jnp.int32, (ROWS, BOX), 1)
+    rows = rows_of(own_ref)
+    columns = columns_of(own_ref)
     sums = [zeros(), zeros()]
-    for s in range(2):
-        products = [
-            lax.dot_general(box_of(own_ref, s), weights_ref[b], NN, preferred_element_type=F32) for b in range(2)
-        ]
-        mine = [targets(rows, b, (0.0, float(s - b), 0.0)) for b in range(2)]
+    for s, b in ((1, 0), (0, 0), (1, 1)):
+        product = lax.dot_general(box_of(own_ref, s), weights_ref[b], NN, preferred_element_type=F32)
+        mine = targets(rows, b, (0.0, float(s - b), 0.0))
         for r in range(0, BOX, ROWS):
-            theirs = sources(columns, s, r)
-            for b in range(2):
-                along = [t - m for t, m in zip(theirs, mine[b], strict=True)]
-                strength = strengths(*along, tile(products[b], r))
-                sums[b] = [t + strength * a for t, a in zip(sums[b], along, strict=True)]
-    return [jnp.concatenate([total(sums[0][c]), total(sums[1][c])], axis=0) for c in range(3)]
+            along = [t - m for t, m in zip(sources(columns, s, r), mine, strict=True)]
+            strength = strengths(*along, tile(product, r))
+            terms = [strength * a for a in along]
+            sums[b] = [t + u for t, u in zip(sums[b], terms, strict=True)]
+            if s != b:
+                x, y, z = [jnp.sum(t, axis=1, keepdims=True) * -SCALE for t in terms]
+                turned[r : r + ROWS, :] = jnp.where(lane == 0, x, jnp.where(lane == 1, y, z))
+    back = jnp.transpose(turned[...])
+    return [
+        jnp.concatenate([total(sums[0][c]), total(sums[1][c]) + back[c : c + 1]], axis=0) for c in range(3)
+    ]
 
 
 def across(own_ref, outer_ref, before_ref, w_filter_ref, so_far_ref, forces_ref, back_ref, filtered, turned):
@@ -246,8 +251,8 @@
     return [jnp.concatenate([total(sums[0][c]), total(sums[1][c])], axis=0) for c in range(3)]
 
 
-def column(own_ref, outer_ref, weights_ref, forces_ref):
-    near, far = within(own_ref, weights_ref), outer_pairs(own_ref, outer_ref, weights_ref, 0.0)
+def column(own_ref, outer_ref, weights_ref, forces_ref, turned):
+    near, far = within(own_ref, weights_ref, turned), outer_pairs(own_ref, outer_ref, weights_ref, 0.0)
     for c in range(3):
         forces_ref[c] = near[c] + far[c]
 
@@ -320,7 +325,7 @@
     weights = kernel(spread, "spread", shape(2, 2 * F, RADIAL * BOX, dtype=BF16), 2, 0)(own, filters)
     outer = kernel(join, "join", shape(2 * BOX + TAIL, 2 * F, dtype=BF16), 3)(second, first, weights)
     before_outer = pass_on(outer, "plane", 1)
-    forces = kernel(column, "column", forces_shape, 3, 2)(own, outer, weights)
+    forces = kernel(column, "column", forces_shape, 3, 2, [pltpu.VMEM((BOX, BOX), F32)])(own, outer, weights)
     forces, back = kernel(
         across,
         "across",

time: 32.2 us -> 32.3 us (level)
  no operation moved by 1% of the time
where the time goes in v5:
time: 32.3 us; the launch traced here: 32 us
  starting transfers between devices  25.1 us (78%)
  Pallas kernels  6.07 us (19%)
  waiting for transfers between devices  0.76 us (2%)
    ppermute x3, starting transfers between devices, pass_on(): return lax.ppermute(x, axis, [(i, (i + step) % n) for i in range(n)])  15.2 us
    ppermute x2, starting transfers between devices, swap(): return lax.ppermute(x, axis, perm)  9.85 us
    pallas_call x1, Pallas kernels, on_device(): kernel(across, 'across', (forces_shape, forces_shape), 5, 8, [pltpu.VMEM(...  1.65 us
    pallas_call x1, Pallas kernels, on_device(): pl.pallas_call(prepare, out_shape=(shape(2 * BOX + TAIL, 2 * F, dtype=BF1...  1.49 us
    pallas_call x1, Pallas kernels, on_device(): kernel(column, 'column', forces_shape, 3, 2, [pltpu.VMEM((BOX, BOX), F32)])  1.14 us
  transfers between devices with their start and end apart: 5, of which 2 were waited for; matrix products, arithmetic and copies ran while one was open for 0% of the time, Pallas kernels for 13%

profile of v5, /device:TPU:1, one launch (start us, length us, event | category | flops | bytes accessed | tf_op | source)
XLA Modules:
  0.0 32.0 jit_solution(15229136926978415583)
XLA Ops:
  0.0 1.5 %prepare.1 = (bf16[264,512]{1,0:T(8,128)(2,1)S(1)}, bf16[136,512]{1,0:T(8,128)(2,1)S(1)}, bf16[136,512]{1,0:T(8,128)(2,1)S(1)}, bf16[8,256]{1,0:T(8,128)(2,1)S(1)}) custom-call(s32[1,2]{1,0:T(1,128)} %counts_ref.1, bf16[3,2,128]{2,1,0:T(2,128)(2,1)} %bitcast.10, bf16[2,128,256]{2,1,0:T(8,128)(2,1)} %bitcast.8, bf16[2,128,256]{2,1,0:T(8,128)(2,1)} %bitcast.9, ...), custom_call_target="tpu_custom_call" | custom-call | tf_op jit(solution)/shard_map/prepare/pallas_call | solution.py:300
  1.5 7.9 %collective-permute-start = (bf16[136,512]{1,0:T(8,128)(2,1)S(1)}, bf16[136,512]{1,0:T(8,128)(2,1)S(1)}, u32[]{:S(2)}, u32[]{:S(2)}) collective-permute-start(bf16[136,512]{1,0:T(8,128)(2,1)S(1)} %get-tuple-element.12), channel_id=1, source_target_pairs={{0,7},{1,2},{2,1},{3,4},{4,3},{5,6},{6,5},{7,0},{8,15},{9,10},{10,... | collective-permute-start | bytes 417800 | tf_op jit(solution)/shard_map/ppermute | solution.py:276
  9.4 1.9 %collective-permute-start.1 = (bf16[136,512]{1,0:T(8,128)(2,1)S(1)}, bf16[136,512]{1,0:T(8,128)(2,1)S(1)}, u32[]{:S(2)}, u32[]{:S(2)}) collective-permute-start(bf16[136,512]{1,0:T(8,128)(2,1)S(1)} %get-tuple-element.13), channel_id=1, source_target_pairs={{0,1},{1,0},{2,3},{3,2},{4,5},{5,4},{6,7},{7,6},{8,9},{9,8},{10,11... | collective-permute-start | bytes 417800 | tf_op jit(solution)/shard_map/ppermute | solution.py:276
  11.4 3.1 %collective-permute-start.3 = (bf16[264,512]{1,0:T(8,128)(2,1)S(1)}, bf16[264,512]{1,0:T(8,128)(2,1)S(1)}, u32[]{:S(2)}, u32[]{:S(2)}) collective-permute-start(bf16[264,512]{1,0:T(8,128)(2,1)S(1)} %get-tuple-element.11.own_ref), channel_id=1, source_target_pairs={{0,8},{8,16},{16,24},{24,32},{32,40},{40,48},{48,56},{56,64},{64,7... | collective-permute-start | bytes 811016 | tf_op jit(solution)/shard_map/ppermute | solution.py:281
  14.4 0.6 %spread.1.weights_ref = bf16[2,512,1024]{2,1,0:T(8,128)(2,1)S(1)} custom-call(bf16[264,512]{1,0:T(8,128)(2,1)S(1)} %get-tuple-element.11.own_ref, bf16[8,256]{1,0:T(8,128)(2,1)S(1)} %get-tuple-element.14.w_filter_ref), custom_call_target="tpu_custom_call" | custom-call | bytes 262144 | tf_op jit(solution)/shard_map/spread/pallas_call | solution.py:325
  15.0 0.0 collective-permute-done.second_ref
  15.0 0.5 %collective-permute-done.1.first_ref = bf16[136,512]{1,0:T(8,128)(2,1)S(1)} collective-permute-done((bf16[136,512]{1,0:T(8,128)(2,1)S(1)}, bf16[136,512]{1,0:T(8,128)(2,1)S(1)}, u32[]{:S(2)}, u32[]{:S(2)}) %collective-permute-start.1) | collective-permute-done | bytes 139296 | tf_op jit(solution)/shard_map/ppermute | solution.py:276
  15.6 0.1 join.1.outer_ref
  15.6 4.0 %collective-permute-start.2 = (bf16[264,512]{1,0:T(8,128)(2,1)S(1)}, bf16[264,512]{1,0:T(8,128)(2,1)S(1)}, u32[]{:S(2)}, u32[]{:S(2)}) collective-permute-start(bf16[264,512]{1,0:T(8,128)(2,1)S(1)} %join.1.outer_ref), channel_id=1, source_target_pairs={{0,8},{8,16},{16,24},{24,32},{32,40},{40,48},{48,56},{56,64},{64,7... | collective-permute-start | bytes 811016 | tf_op jit(solution)/shard_map/ppermute | solution.py:281
  19.6 1.1 %column.1.so_far_ref = f32[3,2,128]{2,1,0:T(2,128)S(1)} custom-call(bf16[264,512]{1,0:T(8,128)(2,1)S(1)} %get-tuple-element.11.own_ref, bf16[264,512]{1,0:T(8,128)(2,1)S(1)} %join.1.outer_ref, bf16[2,512,1024]{2,1,0:T(8,128)(2,1)S(1)} %spread.1.weights_ref), custom_call_target="tpu_custom_call" | custom-call | flops 268435456 | bytes 262144 | tf_op jit(solution)/shard_map/column/pallas_call | solution.py:328
  20.8 0.0 collective-permute-done.3.before_ref
  20.8 1.7 %across.1 = (f32[3,2,128]{2,1,0:T(2,128)S(1)}, f32[3,2,128]{2,1,0:T(2,128)S(1)}) custom-call(bf16[264,512]{1,0:T(8,128)(2,1)S(1)} %get-tuple-element.11.own_ref, bf16[264,512]{1,0:T(8,128)(2,1)S(1)} %join.1.outer_ref, bf16[264,512]{1,0:T(8,128)(2,1)S(1)} %collective-permute-done.3.before_ref, bf16[8,256]{1,0:T(8,128)(2,1)S(1)} %get-tuple-element.14.w_filter_ref, ...), custom_call_target="tpu_custom_call" | custom-call | flops 1073741824 | bytes 262144 | tf_op jit(solution)/shard_map/across/pallas_call | solution.py:329
  22.4 8.2 %collective-permute-start.4 = (f32[3,2,128]{2,1,0:T(2,128)S(1)}, f32[3,2,128]{2,1,0:T(2,128)S(1)}, u32[]{:S(2)}, u32[]{:S(2)}) collective-permute-start(f32[3,2,128]{2,1,0:T(2,128)S(1)} %get-tuple-element.16), channel_id=1, source_target_pairs={{0,504},{8,0},{16,8},{24,16},{32,24},{40,32},{48,40},{56,48},{64,5... | collective-permute-start | bytes 9224 | tf_op jit(solution)/shard_map/ppermute | solution.py:281
  30.6 0.0 collective-permute-done.2.outer_ref
  30.6 0.6 %corner.1.so_far_ref = f32[3,2,128]{2,1,0:T(2,128)S(1)} custom-call(bf16[264,512]{1,0:T(8,128)(2,1)S(1)} %get-tuple-element.11.own_ref, bf16[264,512]{1,0:T(8,128)(2,1)S(1)} %collective-permute-done.2.outer_ref, bf16[2,512,1024]{2,1,0:T(8,128)(2,1)S(1)} %spread.1.weights_ref, f32[3,2,128]{2,1,0:T(2,128)S(1)} %get-tuple-element.15.so_far_ref), custom_call_target="tpu_custom_call" | custom-call | flops 268435456 | bytes 262144 | tf_op jit(solution)/shard_map/corner/pallas_call | solution.py:338
  31.2 0.2 collective-permute-done.4.returned_ref
  31.4 0.6 %finish.1 = f32[3,2,128]{2,1,0:T(2,128)} custom-call(f32[3,2,128]{2,1,0:T(2,128)S(1)} %corner.1.so_far_ref, f32[3,2,128]{2,1,0:T(2,128)S(1)} %collective-permute-done.4.returned_ref), custom_call_target="tpu_custom_call" | custom-call | bytes 262144 | tf_op jit(solution)/shard_map/finish/pallas_call | solution.py:339
Async XLA Ops:
  1.5 13.5 %collective-permute-start = (bf16[136,512]{1,0:T(8,128)(2,1)S(1)}, bf16[136,512]{1,0:T(8,128)(2,1)S(1)}, u32[]{:S(2)}, u32[]{:S(2)}) collective-permute-start(bf16[136,512]{1,0:T(8,128)(2,1)S(1)} %get-tuple-element.12), channel_id=1, source_target_pairs={{0,7},{1,2},{2,1},{3,4},{4,3},{5,6},{6,5},{7,0},{8,15},{9,10},{10,... | collective-permute-start | bytes 417800 | tf_op jit(solution)/shard_map/ppermute | solution.py:276
  9.4 6.1 %collective-permute-start.1 = (bf16[136,512]{1,0:T(8,128)(2,1)S(1)}, bf16[136,512]{1,0:T(8,128)(2,1)S(1)}, u32[]{:S(2)}, u32[]{:S(2)}) collective-permute-start(bf16[136,512]{1,0:T(8,128)(2,1)S(1)} %get-tuple-element.13), channel_id=1, source_target_pairs={{0,1},{1,0},{2,3},{3,2},{4,5},{5,4},{6,7},{7,6},{8,9},{9,8},{10,11... | collective-permute-start | bytes 417800 | tf_op jit(solution)/shard_map/ppermute | solution.py:276
  11.4 9.4 %collective-permute-start.3 = (bf16[264,512]{1,0:T(8,128)(2,1)S(1)}, bf16[264,512]{1,0:T(8,128)(2,1)S(1)}, u32[]{:S(2)}, u32[]{:S(2)}) collective-permute-start(bf16[264,512]{1,0:T(8,128)(2,1)S(1)} %get-tuple-element.11.own_ref), channel_id=1, source_target_pairs={{0,8},{8,16},{16,24},{24,32},{32,40},{40,48},{48,56},{56,64},{64,7... | collective-permute-start | bytes 811016 | tf_op jit(solution)/shard_map/ppermute | solution.py:281
  15.6 15.0 %collective-permute-start.2 = (bf16[264,512]{1,0:T(8,128)(2,1)S(1)}, bf16[264,512]{1,0:T(8,128)(2,1)S(1)}, u32[]{:S(2)}, u32[]{:S(2)}) collective-permute-start(bf16[264,512]{1,0:T(8,128)(2,1)S(1)} %join.1.outer_ref), channel_id=1, source_target_pairs={{0,8},{8,16},{16,24},{24,32},{32,40},{40,48},{48,56},{56,64},{64,7... | collective-permute-start | bytes 811016 | tf_op jit(solution)/shard_map/ppermute | solution.py:281
  22.4 9.0 %collective-permute-start.4 = (f32[3,2,128]{2,1,0:T(2,128)S(1)}, f32[3,2,128]{2,1,0:T(2,128)S(1)}, u32[]{:S(2)}, u32[]{:S(2)}) collective-permute-start(f32[3,2,128]{2,1,0:T(2,128)S(1)} %get-tuple-element.16), channel_id=1, source_target_pairs={{0,504},{8,0},{16,8},{24,16},{32,24},{40,32},{48,40},{56,48},{64,5... | collective-permute-start | bytes 9224 | tf_op jit(solution)/shard_map/ppermute | solution.py:281
